TPU v7x, 128 devices: a whole 4x4x4 slice. The times are simulated.
128 devices in a mesh: group: 2 (over core), gx: 8 (over z_lo, x), gy: 8 (over z_hi, y).
Axes of the slice: x: 4, y: 4, z: 4 (z_hi: 2, z_lo: 2; z = z_hi * 2 + z_lo), core: 2. Of those that a mesh axis runs over, the one named last changes fastest.
Arguments:
- state: float32 [2, 3, 128, 256, 128], P('group', None, 'gx', 'gy'), may hold values from -6 to 6
- conduct: float32 [2, 3, 3, 128, 256, 128], P('group', None, None, 'gx', 'gy'), may hold values from 0.1 to 10
- capacity: float32 [2, 128, 256, 128], P('group', 'gx', 'gy'), may hold values from 0.3 to 3
- supply: float32 [2, 3, 128, 256, 128], P('group', None, 'gx', 'gy'), may hold values from -10.5 to 13.5
- flags: int32 [128, 256], P('gx', 'gy'), may hold values 0 or 1
- layer_map: int32 [384], replicated, may hold values from 0 to 127, never falling along the last dimension, each value on 1 to 6 neighbouring positions
Outputs:
- new_state: float32 [2, 3, 128, 256, 128], P('group', None, 'gx', 'gy')
- balance: float32 [2], replicated
Inputs may be any that keep to these rules, and one draw needn't show every extreme that they name: `layer_map`: never falls; every brick layer holds 1 to 6 fine layers, one exactly 6.
All inputs are finite; a program needn't handle non-finite values. No bound on the sum of `flags` on one device may be relied on, other than what follows from the above.
Results may differ from a plain program's by a relative error of at most 0.0001.
Values sent between devices are 32-bit elements; how exact they have to be, the bound alone decides.
No kernel may reach another device: no remote copies, remote signals or barrier semaphores. Data moves between devices by JAX's collectives and lax.ppermute only.
A program may use at most 128 MiB of HBM per device.

v0:
```python
import jax
import jax.numpy as jnp
from jax import lax
from jax.experimental import pallas as pl
from jax.experimental.pallas import tpu as pltpu
from jax.sharding import PartitionSpec as P

AXES = ("group", "gx", "gy")
X, Y, Z = 16, 32, 128
OX, OY = 3, 4
EX, EY = X + 2 * OX, Y + 2 * OY
BETA = 0.5
BIOT = 0.8
F32 = jnp.float32

X_ROWS = [(f, r) for f in range(13) for r in range(1, (3 if f < 3 else 2 if f < 10 else 1) + 1)]
Y_ROWS = [
    (f, r) for f in range(13) for r in range(1, (3 if 3 <= f < 6 else 2 if f < 10 else 1) + 1)
]
CORNER = [(1, 1), (1, 2), (2, 1), (2, 2), (1, 3), (3, 1)]
K_CORNERS = (
    [(f, i, j) for f in range(3) for i, j in CORNER[:4] + [(3, 1)]]
    + [(f, i, j) for f in range(3, 6) for i, j in CORNER[:4] + [(1, 3)]]
    + [(f, i, j) for f in range(6, 10) for i, j in CORNER[:3]]
)
R_ROWS = [(f, r) for f in range(3) for r in range(1, 4)]
R_CORNERS = [(f, i, j) for f in range(3) for i, j in CORNER]
AT_R = [len(R_ROWS) * X, len(R_ROWS) * X + len(R_CORNERS)]
AT_K = [AT_R[1] + len(R_CORNERS), AT_R[1] + len(R_CORNERS) + len(K_CORNERS)]
AT_Q = [AT_K[1] + len(K_CORNERS), AT_K[1] + len(K_CORNERS) + 3]
AT_U = AT_Q[1] + 3
Y_PACK = -(-(AT_U + 4) // 8) * 8
Q_SLOT = [R_ROWS.index((0, 3)), R_ROWS.index((1, 3))]


def struct(*shape):
    return jax.ShapeDtypeStruct(shape, F32)


def call(kernel, outs, scratch=(), left=(), count=0, cost=None, limit=20, scalars=()):
    extra = {}
    if left:
        extra["in_specs"] = [
            pl.BlockSpec(memory_space=pltpu.HBM if n in left else pltpu.VMEM) for n in range(count)
        ]
    if scalars:
        extra["out_specs"] = [
            pl.BlockSpec(memory_space=pltpu.SMEM if n in scalars else pltpu.VMEM)
            for n in range(len(outs))
        ]
    if cost:
        extra["cost_estimate"] = pl.CostEstimate(
            flops=cost, bytes_accessed=cost, transcendentals=0
        )
    return pl.pallas_call(
        kernel,
        out_shape=outs,
        scratch_shapes=list(scratch),
        compiler_params=pltpu.CompilerParams(vmem_limit_bytes=limit << 20),
        **extra,
    )


def up_y(v):
    return pltpu.roll(v, v.shape[0] - 1, 0)


def down_y(v):
    return pltpu.roll(v, 1, 0)


def up_z(v):
    return pltpu.roll(v, Z - 1, 1)


def down_z(v):
    return pltpu.roll(v, 1, 1)


def lanes(rows):
    return lax.broadcasted_iota(jnp.int32, (rows, Z), 1)


def rows_of(rows):
    return lax.broadcasted_iota(jnp.int32, (rows, Z), 0)


def to_tile(v):
    return pltpu.roll(v, EY - OY, 0)[:Y]


def harmonic(a, b):
    return 2.0 * a * b / jnp.maximum(a + b, 1e-30)


def one_hot(map_ref):
    brick = lax.broadcasted_iota(jnp.int32, (Z, 3 * Z), 0)
    return jnp.where(brick == map_ref[...], 1.0, 0.0).astype(jnp.bfloat16)


def dot_split(v, hot, contract):
    high = v.astype(jnp.bfloat16)
    low = (v - high.astype(F32)).astype(jnp.bfloat16)
    dims = (((1,), (contract,)), ((), ()))
    return lax.dot_general(high, hot, dims, preferred_element_type=F32) + lax.dot_general(
        low, hot, dims, preferred_element_type=F32
    )


def spread(v, hot, k):
    return dot_split(v, hot[:, k * Z : (k + 1) * Z], 0)


def gather_up(parts, hot):
    total = None
    for k, v in enumerate(parts):
        part = dot_split(v, hot[:, k * Z : (k + 1) * Z], 1)
        total = part if total is None else total + part
    ones = jnp.ones((8, 3 * Z), jnp.bfloat16)
    counts = lax.dot_general(ones, hot, (((1,), (1,)), ((), ())), preferred_element_type=F32)
    return total * (1.0 / counts[:1])


def gather_wide(ref, hot):
    rows = EX - 2
    parts = [ref[k, 1 : EX - 1].reshape(rows * EY, Z) for k in range(3)]
    return gather_up(parts, hot).reshape(rows, EY, Z)


def fetch(pairs, sem, start=0):
    copies = [pltpu.make_async_copy(a, b, sem.at[start + n]) for n, (a, b) in enumerate(pairs)]
    for copy in copies:
        copy.start()
    return copies


class Either:
    def __init__(self, odd, at_odd, at_even):
        self.odd, self.at_odd, self.at_even = odd, at_odd, at_even

    def __getitem__(self, at):
        return jnp.where(self.odd, self.at_odd[at], self.at_even[at])


def parity(axis):
    return lax.rem(lax.axis_index(axis), 2) == 1


def lower_upper(axis, first, second):
    odd = parity(axis)
    return Either(odd, first, second), Either(odd, second, first)


def surroundings(xa, xb, ya, yb):
    return lower_upper("gx", xa, xb) + lower_upper("gy", ya, yb)


def put(first, second, at, odd, tail, head):
    first[at] = jnp.where(odd, head, tail)
    second[at] = jnp.where(odd, tail, head)


def pack_x(source, rows, first, second):
    odd = parity("gx")
    for n, (f, r) in enumerate(rows):
        put(first, second, n, odd, source(f)[X - r], source(f)[r - 1])


def unpack_x(target, rows, low, up):
    for n, (f, r) in enumerate(rows):
        target(f)[OX - r, OY : OY + Y] = low[n]
        target(f)[OX + X - 1 + r, OY : OY + Y] = up[n]


def corner_at(side, i, j):
    row = OX - i if side[0] == 0 else OX + X - 1 + i
    column = OY - j if side[1] == 0 else OY + Y - 1 + j
    return row, slice(column, column + 1)


def x_faces(rows):
    return [struct(len(rows), Y, Z)] * 2


def loop(first, last, body, init=0, unroll=4):
    steps = (last - first) // unroll

    def step(n, carry):
        for m in range(unroll):
            carry = body(first + n * unroll + m, carry)
        return carry

    init = lax.fori_loop(0, steps, step, init)
    for i in range(first + steps * unroll, last):
        init = body(i, init)
    return init


def vertical_faces(conduct, flags, bottom, store):
    flow = lax.axis_index("group") == 0
    last = lanes(Y) == Z - 1
    eye = jnp.where(
        lax.broadcasted_iota(jnp.int32, (Y, Y), 0) == lax.broadcasted_iota(jnp.int32, (Y, Y), 1),
        1.0,
        0.0,
    ).astype(jnp.bfloat16)
    columns = lax.dot_general(
        eye,
        flags[...].astype(F32).astype(jnp.bfloat16),
        (((1,), (1,)), ((), ())),
        preferred_element_type=F32,
    )
    for x in range(X):
        bottom[x] = jnp.broadcast_to(columns[:, x : x + 1], (Y, Z))

    def row(x, carry):
        kz = [conduct[2, k, x] for k in range(3)]
        rolled = [up_z(v) for v in kz]
        ends = [rolled[1], rolled[2], bottom[x] * kz[2]]
        for k in range(3):
            end = jnp.where(flow, ends[k], kz[k])
            store(x, k, harmonic(kz[k], jnp.where(last, end, rolled[k])))
        return carry

    loop(0, X, row)


def pack_kernel(flags_in, state_in, conduct_in, capacity_in, xa, xb, ya, yb, *scratch):
    flags, state, conduct, capacity, bottom, tz, sem = scratch
    early = [(flags_in, flags)] + [(conduct_in.at[2, k], conduct.at[2, k]) for k in range(3)]
    late = [(conduct_in.at[d, k], conduct.at[d, k]) for d in range(2) for k in range(3)]
    late += [(state_in.at[k], state.at[k]) for k in range(3)] + [(capacity_in, capacity)]
    early = fetch(early, sem)
    late = fetch(late, sem, len(early))
    for copy in early:
        copy.wait()
    def store(x, k, value):
        tz[k, x] = value

    vertical_faces(conduct, flags, bottom, store)
    for copy in late:
        copy.wait()

    def source(f):
        if f < 6:
            return conduct.at[f // 3, f % 3]
        if f < 9:
            return tz.at[f - 6]
        return capacity if f == 9 else state.at[f - 10]

    pack_x(source, X_ROWS, xa, xb)
    odd = parity("gy")
    for n, (f, r) in enumerate(Y_ROWS):
        put(ya, yb, n, odd, source(f)[:, Y - r, :], source(f)[:, r - 1, :])


class Faces:
    def __init__(self, x, y, z, own):
        self.x, self.y, self.z, self.own = x, y, z, own


def faces_in(ref, shift=0):
    return Faces(*[lambda c, i, d=d: ref[3 * d + c, i - shift] for d in range(4)])


def lateral(faces, v_ref, c, i, v, fx_before):
    fx = faces.x(c, i) * (v - v_ref[c, i + 1])
    fy = faces.y(c, i) * (v - up_y(v))
    return (fx - fx_before) + (fy - down_y(fy)), fx


def x_flux(faces, v_ref, i):
    return tuple(faces.x(c, i) * (v_ref[c, i] - v_ref[c, i + 1]) for c in range(3))


def flow_below(vs, last):
    rolled = [up_z(v) for v in vs]
    ends = [rolled[1], rolled[2], 0.0]
    return [jnp.where(last, ends[k], rolled[k]) for k in range(3)]


def flow_row(faces, v_ref, i, fx_before):
    last, first = lanes(EY) == Z - 1, lanes(EY) == 0
    vs = [v_ref[k, i] for k in range(3)]
    below = flow_below(vs, last)
    fz = [faces.z(k, i) * (vs[k] - below[k]) for k in range(3)]
    moved = [down_z(v) for v in fz]
    ends = [0.0, moved[0], moved[1]]
    out, fx_now = [], []
    for k in range(3):
        side, fx = lateral(faces, v_ref, k, i, vs[k], fx_before[k])
        above = jnp.where(first, ends[k], moved[k])
        out.append(faces.own(k, i) * vs[k] + side + (fz[k] - above))
        fx_now.append(fx)
    return out, tuple(fx_now)


def strain_row(v_ref, i):
    v0, v1, v2 = v_ref[0, i], v_ref[1, i], v_ref[2, i]
    low = jnp.where(lanes(EY) == Z - 1, 0.0, up_z(v2))
    return (v_ref[0, i + 1] - v0) + (up_y(v1) - v1) + (low - v2)


def solid_row(faces, v_ref, i, s_before, fx_before):
    last, first = lanes(EY) == Z - 1, lanes(EY) == 0
    e = strain_row(v_ref, i)
    s = faces.own(0, i) * e
    grad = [s_before - s, down_y(s) - s, jnp.where(first, 0.0, down_z(s)) - s]
    out, fx_now = [], []
    for c in range(3):
        v = v_ref[c, i]
        side, fx = lateral(faces, v_ref, c, i, v, fx_before[c])
        fz = faces.z(c, i) * (v - jnp.where(last, 0.0, up_z(v)))
        above = jnp.where(first, 0.0, down_z(fz))
        out.append((side + (fz - above)) + grad[c])
        fx_now.append(fx)
    return out, s, tuple(fx_now)


BESIDE = [(1, -1, Y), (1, X - 1, Y), (1, -1, 0), (1, X - 1, 0)]
BESIDE += [(0, X, -1), (0, 0, -1), (0, X, Y - 1), (0, 0, Y - 1)]


def place_tile(conduct, capacity, keep, caps):
    at = slice(OY, OY + Y)

    def row(x, carry):
        for f in range(6):
            keep[f, OX + x, at] = conduct[f // 3, f % 3, x]
        caps[OX + x, at] = capacity[x]
        return carry

    loop(0, X, row)


def interior_kernel(state, conduct, capacity, flags, layer_map, faces, tz, unit, keep, caps, bottom):
    flow = lax.axis_index("group") == 0
    place_tile(conduct, capacity, keep, caps)

    def store(x, k, value):
        tz[k, x] = value
        faces[6 + k, OX + x, OY : OY + Y] = value

    vertical_faces(conduct, flags, bottom, store)
    loop(OX, OX + X, lambda i, carry: lateral_faces(keep, faces, i))

    @pl.when(flow)
    def _():
        hot = one_hot(layer_map)
        bricks = caps[OX : OX + X].reshape(X * EY, Z)
        for k in range(3):
            faces[9 + k, OX : OX + X] = (spread(bricks, hot, k) + BETA).reshape(X, EY, Z)
        parts = [state[k].reshape(X * Y, Z) for k in range(3)]
        unit[...] = gather_up(parts, hot).reshape(X, Y, Z)


def lateral_faces(keep, faces, i):
    for c in range(3):
        faces[c, i] = harmonic(keep[c, i], keep[c, i + 1])
        here = keep[3 + c, i]
        faces[3 + c, i] = harmonic(here, up_y(here))
    return 0


def strain_kernel(state, unit, xa, xb, ya, yb, strain):
    flow = lax.axis_index("group") == 0
    _, xu, _, yu = surroundings(xa, xb, ya, yb)

    @pl.when(flow)
    def _():
        strain[...] = unit[...]

    @pl.when(jnp.logical_not(flow))
    def _():
        last = lanes(Y) == Z - 1
        edge = rows_of(Y) == Y - 1
        n_x, n_y = X_ROWS.index((10, 1)), Y_ROWS.index((11, 1))
        for x in range(X):
            v0, v1, v2 = (state[c, x] for c in range(3))
            east = state[0, x + 1] if x + 1 < X else xu[n_x]
            north = jnp.where(edge, yu[n_y, x : x + 1], up_y(v1))
            low = jnp.where(last, 0.0, up_z(v2))
            strain[x] = (east - v0) + (north - v1) + (low - v2)


def first_kernel(state, conduct, capacity, supply, faces_ref, xa, xb, ya, yb, *refs):
    xl, xu, yl, yu = surroundings(xa, xb, ya, yb)
    base, beside, sides, own, field = refs
    flow = lax.axis_index("group") == 0

    def place(x, carry):
        for c in range(3):
            field[c, OX + x, OY : OY + Y] = state[c, x]
        for f in range(6):
            sides[f, OX + x] = faces_ref[f, OX + x]
        return carry

    loop(0, X, place)
    for c in range(3):
        n = X_ROWS.index((10 + c, 1))
        field[c, OX - 1, OY : OY + Y] = xl[n]
        field[c, OX + X, OY : OY + Y] = xu[n]
        n = Y_ROWS.index((10 + c, 1))
        field[c, OX : OX + X, OY - 1, :] = yl[n]
        field[c, OX : OX + X, OY + Y, :] = yu[n]
        n = X_ROWS.index((c, 1))
        at = slice(OY, OY + Y)
        sides[c, OX - 1, at] = harmonic(xl[n], conduct[0, c, 0])
        sides[c, OX + X - 1, at] = harmonic(conduct[0, c, X - 1], xu[n])
        n = Y_ROWS.index((3 + c, 1))
        sides[3 + c, OX : OX + X, OY - 1, :] = harmonic(yl[n], conduct[1, c, :, 0, :])
        sides[3 + c, OX : OX + X, OY + Y - 1, :] = harmonic(conduct[1, c, :, Y - 1, :], yu[n])
    field[1, OX - 1, OY + Y : OY + Y + 1] = jnp.zeros((1, Z), F32)
    field[0, OX + X, OY - 1 : OY] = jnp.zeros((1, Z), F32)
    for n, (c, x, y) in enumerate(BESIDE):
        beside[n : n + 1] = field[c, OX + x, OY + y : OY + y + 1]
    inner = faces_in(faces_ref)
    outer = faces_in(sides)

    @pl.when(flow)
    def _():
        faces = Faces(outer.x, outer.y, inner.z, inner.own)

        def row(i, fx_before):
            image, fx = flow_row(faces, field, i, fx_before)
            for k in range(3):
                base[k, i - OX] = (
                    supply[k, i - OX] + BETA * state[k, i - OX] - to_tile(image[k])
                )
            return fx

        loop(OX, OX + X, row, x_flux(faces, field, OX - 1))

    @pl.when(jnp.logical_not(flow))
    def _():
        def place(x, carry):
            own[OX + x, OY : OY + Y] = capacity[x]
            return carry

        loop(0, X, place)
        own[OX - 1, OY : OY + Y] = xl[X_ROWS.index((9, 1))]
        own[OX : OX + X, OY - 1, :] = yl[Y_ROWS.index((9, 1))]
        faces = Faces(outer.x, outer.y, inner.z, lambda c, i: own[i])

        def row(i, carry):
            image, s, fx = solid_row(faces, field, i, carry[0], carry[1])
            for c in range(3):
                base[c, i - OX] = supply[c, i - OX] - to_tile(image[c])
            return s, fx

        before = faces.own(0, OX - 1) * strain_row(field, OX - 1)
        loop(OX, OX + X, row, (before, x_flux(faces, field, OX - 1)))


def halo_kernel(conduct, capacity, tz, layer_map, xa, xb, ya, yb, faces, rim, keep, caps):
    xl, xu, yl, yu = surroundings(xa, xb, ya, yb)
    flow = lax.axis_index("group") == 0

    def target(f):
        if f < 6:
            return keep.at[f]
        return faces.at[f] if f < 9 else caps

    place_tile(conduct, capacity, keep, caps)

    def place(x, carry):
        for k in range(3):
            faces[6 + k, OX + x, OY : OY + Y] = tz[k, x]
        return carry

    loop(0, X, place)
    for n, (f, r) in enumerate(X_ROWS):
        if f < 10:
            target(f)[OX - r, OY : OY + Y] = xl[n]
            target(f)[OX + X - 1 + r, OY : OY + Y] = xu[n]
    for n, (f, r) in enumerate(Y_ROWS):
        if f < 10:
            target(f)[OX : OX + X, OY - r, :] = yl[n]
            target(f)[OX : OX + X, OY + Y - 1 + r, :] = yu[n]
    loop(0, EX - 1, lambda i, carry: lateral_faces(keep, faces, i))
    for n, i in enumerate(K_RIM):
        for f in range(6):
            rim[f, n] = keep[f, i]

    @pl.when(flow)
    def _():
        hot = one_hot(layer_map)
        bricks = caps[1 : EX - 1].reshape((EX - 2) * EY, Z)
        for k in range(3):
            faces[9 + k, 1 : EX - 1] = (spread(bricks, hot, k) + BETA).reshape(EX - 2, EY, Z)

    @pl.when(jnp.logical_not(flow))
    def _():
        faces[9] = caps[...]


BESIDE = [(1, -1, Y), (1, X - 1, Y), (1, -1, 0), (1, X - 1, 0)]
BESIDE += [(0, X, -1), (0, 0, -1), (0, X, Y - 1), (0, 0, Y - 1)]
RIM = [0, 1, 2, EX - 4, EX - 3, EX - 2]
K_RIM = [0, 1, 2, 3, EX - 4, EX - 3, EX - 2, EX - 1]


def residual_kernel(base, strain, unit, layer_map, residual, xa, xb):
    flow = lax.axis_index("group") == 0

    @pl.when(flow)
    def _():
        hot = one_hot(layer_map)
        e = strain[...].reshape(X * Y, Z)
        for k in range(3):
            residual[k] = base[k] - BIOT * spread(e, hot, k).reshape(X, Y, Z)

    @pl.when(jnp.logical_not(flow))
    def _():
        residual[...] = base[...]

    pack_x(lambda f: residual.at[f], R_ROWS, xa, xb)

    @pl.when(jnp.logical_not(flow))
    def _():
        odd = parity("gx")
        for depth, n in enumerate(Q_SLOT):
            put(xa, xb, n, odd, unit[X - 1 - depth], unit[depth])


def relay_kernel(residual, unit, xa, xb, ka, kb, ya, yb):
    flow = lax.axis_index("group") == 0
    odd = parity("gy")
    r_halos, k_halos = lower_upper("gx", xa, xb), lower_upper("gx", ka, kb)

    def give(at, count, ref, index, j):
        put(ya, yb, slice(at, at + count), odd, ref[index(Y - j)], ref[index(j - 1)])

    for n, (f, r) in enumerate(R_ROWS):
        give(n * X, X, residual, lambda y: (f, slice(None), y), r)
    for side in range(2):
        r_halo, k_halo = r_halos[side], k_halos[side]
        for n, (f, i, j) in enumerate(R_CORNERS):
            row = R_ROWS.index((f, i))
            give(AT_R[side] + n, 1, r_halo, lambda y: (row, slice(y, y + 1)), j)
        for n, (f, i, j) in enumerate(K_CORNERS):
            row = X_ROWS.index((f, i))
            give(AT_K[side] + n, 1, k_halo, lambda y: (row, slice(y, y + 1)), j)
        for n, (i, j) in enumerate(CORNER[:3]):
            row = Q_SLOT[i - 1]
            give(AT_Q[side] + n, 1, r_halo, lambda y: (row, slice(y, y + 1)), j)
        for c in range(2):
            row = X_ROWS.index((10 + c, 1))
            give(AT_U + 2 * side + c, 1, k_halo, lambda y: (row, slice(y, y + 1)), 1)

    @pl.when(jnp.logical_not(flow))
    def _():
        for depth, n in enumerate(Q_SLOT):
            give(n * X, X, unit, lambda y: (slice(None), y), depth + 1)


def fold(v):
    return jnp.sum(v.reshape(v.shape[0] // 8, 8, Z), axis=0)


def spread_sums(found):
    lane = lanes(8)
    row = jnp.zeros((8, Z), F32)
    first = rows_of(8) == 0
    for n, total in found.items():
        row = jnp.where(first & (lane == n), jnp.sum(total), row)
    return row


def tile_rows():
    at = rows_of(EY)
    return (at >= OY) & (at < OY + Y)


def fill(residual, target, halos):
    xl, xu, yl, yu = halos

    def place(x, carry):
        for k in range(3):
            target[k, OX + x, OY : OY + Y] = residual[k, x]
        return carry

    loop(0, X, place)
    unpack_x(lambda f: target.at[f], R_ROWS, xl, xu)
    for n, (f, r) in enumerate(R_ROWS):
        target[f, OX : OX + X, OY - r, :] = yl[n * X : (n + 1) * X]
        target[f, OX : OX + X, OY + Y - 1 + r, :] = yu[n * X : (n + 1) * X]
    for v, pack in enumerate((yl, yu)):
        for h in range(2):
            for n, (f, i, j) in enumerate(R_CORNERS):
                row, column = corner_at((h, v), i, j)
                target[f, row, column] = pack[AT_R[h] + n : AT_R[h] + n + 1]


def complete(faces, rim, k_rim_in, k_rim, halos, hot):
    for n, i in enumerate(RIM):
        for f in range(6, 12):
            rim[f, n] = faces[f, i]
    k_rim[...] = k_rim_in[...]
    order = []
    for v, pack in enumerate(halos[2:]):
        for h in range(2):
            for n, (f, i, j) in enumerate(K_CORNERS):
                row, column = corner_at((h, v), i, j)
                value = pack[AT_K[h] + n : AT_K[h] + n + 1]
                if f < 6:
                    k_rim[f, K_RIM.index(row), column] = value
                elif f < 9:
                    rim[f, RIM.index(row), column] = value
                else:
                    order.append((RIM.index(row), column, value))
    for n, i in enumerate(RIM):
        m = K_RIM.index(i)
        for c in range(3):
            rim[c, n] = harmonic(k_rim[c, m], k_rim[c, m + 1])
            here = k_rim[3 + c, m]
            rim[3 + c, n] = harmonic(here, up_y(here))
    if hot is None:
        for row, column, value in order:
            rim[9, row, column] = value
    else:
        values = [value for _, _, value in order]
        values += [jnp.zeros((1, Z), F32)] * (16 - len(values))
        caps = jnp.concatenate(values, axis=0)
        for k in range(3):
            storage = spread(caps, hot, k) + BETA
            for n, (row, column, _) in enumerate(order):
                rim[9 + k, row, column] = storage[n : n + 1]


def row_parts(faces, rim):
    return faces_in(rim), faces_in(faces), faces_in(rim, EX - 7)


def run_rows(parts, first, last, body, init, unroll=3):
    low, middle, high = parts
    for i in range(first, OX):
        init = body(low, i, init)
    init = loop(max(first, OX), EX - 4, lambda i, carry: body(middle, i, carry), init, unroll)
    for i in range(EX - 4, last):
        init = body(high, i, init)
    return init


PAIRS = [(0, 0), (0, 1), (0, 2), (1, 1), (1, 2), (2, 2)]
FIRST_SUM = 9


def grid_mask(before, after):
    gx, gy = lax.axis_index("gx"), lax.axis_index("gy")
    gx_last, gy_last = lax.axis_size("gx") - 1, lax.axis_size("gy") - 1
    at = rows_of(EY)
    in_y = (at >= OY - jnp.where(gy > 0, before, 0)) & (
        at < OY + Y + jnp.where(gy < gy_last, after, 0)
    )

    def in_grid(i):
        in_x = ((i >= OX) | (gx > 0)) & ((i < OX + X) | (gx < gx_last))
        return in_y & in_x

    return in_grid


def load_rows(q_refs, targets, added):
    in_grid = grid_mask(1, 2)

    def row(i, carry):
        for q_ref, target in zip(q_refs, targets):
            load_row(q_ref, target, i, in_grid(i))
        return carry

    def load_row(q_ref, target, i, ok):
        first = lanes(EY) == 0
        q = q_ref[i - 1]
        push = [
            BIOT * (q_ref[i - 2] - q),
            BIOT * (down_y(q) - q),
            BIOT * (jnp.where(first, 0.0, down_z(q)) - q),
        ]
        for c in range(3):
            v = push[c] + target[c, i] if added else push[c]
            target[c, i] = jnp.where(ok, v, 0.0)

    loop(OX - 1, OX + X + 2, row)


def solid_image(parts, f_refs, p_refs, unroll):
    in_grid = grid_mask(0, 1)

    def row(faces, i, carry):
        ok, after = in_grid(i), []
        for f_ref, p_ref, (s, fx) in zip(f_refs, p_refs, carry):
            out, s, fx = solid_row(faces, f_ref, i, s, fx)
            for c in range(3):
                p_ref[c, i] = jnp.where(ok, out[c], 0.0)
            after.append((s, fx))
        return tuple(after)

    view = parts[0]
    start = [
        (view.own(0, OX - 1) * strain_row(f, OX - 1), x_flux(view, f, OX - 1)) for f in f_refs
    ]
    run_rows(parts, OX, OX + X + 1, row, tuple(start), unroll)


def gram_sums(faces, fields, products, pairs, acc):
    acc[...] = jnp.zeros(acc.shape, F32)
    vectors = range(len(fields))

    def row(i, carry):
        inside, last = tile_rows(), lanes(EY) == Z - 1

        def only(v):
            return jnp.where(inside, v, 0.0)

        def add(n, v):
            acc[n] = acc[n] + fold(v)

        strains = [strain_row(p, i) for p in products]
        modulus = only(faces[9, i])
        pushes = [modulus * e for e in strains]
        for n, (a, b) in enumerate(pairs):
            add(4 * n + 3, pushes[a] * strains[b])
        for c in range(3):
            ws = [p[c, i] for p in products]
            dx = [ws[a] - products[a][c, i + 1] for a in vectors]
            dy = [w - up_y(w) for w in ws]
            dz = [w - jnp.where(last, 0.0, up_z(w)) for w in ws]
            sx, sy, sz = (only(faces[3 * d + c, i]) for d in range(3))
            fx = [sx * d for d in dx]
            fy = [sy * d for d in dy]
            fz = [sz * d for d in dz]
            for n, (a, b) in enumerate(pairs):
                add(4 * n + 3, fx[a] * dx[b] + fy[a] * dy[b] + fz[a] * dz[b])
            rs = [only(f[c, i]) for f in fields]
            ws = [only(w) for w in ws]
            for n, (a, b) in enumerate(pairs):
                add(4 * n, rs[a] * rs[b])
                add(4 * n + 1, rs[a] * ws[b])
                add(4 * n + 2, ws[a] * ws[b])
        return carry

    loop(OX, OX + X, row, 0, 2)
    found = {}
    for n, pair in enumerate(pairs):
        for m in range(4):
            found[FIRST_SUM + 6 * m + PAIRS.index(pair)] = acc[4 * n + m]
    return found


def unit_surroundings(unit, halos, q):
    xl, xu, yl, yu = halos

    def place(x, carry):
        q[OX - 1 + x, OY : OY + Y] = unit[x]
        return carry

    loop(0, X, place)
    for depth, n in enumerate(Q_SLOT):
        q[OX - 2 - depth, OY : OY + Y] = xl[n]
        q[OX + X - 1 + depth, OY : OY + Y] = xu[n]
        rows = slice(n * X, (n + 1) * X)
        q[OX - 1 : OX - 1 + X, OY - 1 - depth, :] = yl[rows]
        q[OX - 1 : OX - 1 + X, OY + Y + depth, :] = yu[rows]
    for v, pack in enumerate((yl, yu)):
        for h in range(2):
            for n, (i, j) in enumerate(CORNER[:3]):
                row, column = corner_at((h, v), i, j)
                q[row - 1, column] = pack[AT_Q[h] + n : AT_Q[h] + n + 1]


def late_terms(faces, rim, field, beside, halos):
    yl, yu = halos[2:]

    def modulus(x, y):
        i, column = OX + x, slice(OY + y, OY + y + 1)
        return rim[9, RIM.index(i), column] if i in RIM else faces[9, i, column]

    u1 = [yu[AT_U + 1 : AT_U + 2]] + [beside[n : n + 1] for n in (1, 2, 3)]
    u0 = [yl[AT_U + 2 : AT_U + 3]] + [beside[n : n + 1] for n in (5, 6, 7)]
    for u, (x, y) in zip(u1, ((0, Y - 1), (X, Y - 1), (0, -1), (X, -1))):
        row, column = OX + x, slice(OY + y, OY + y + 1)
        field[0, row, column] = field[0, row, column] - modulus(x - 1, y) * u
    for u, (x, y) in zip(u0, ((X - 1, 0), (-1, 0), (X - 1, Y), (-1, Y))):
        row, column = OX + x, slice(OY + y, OY + y + 1)
        field[1, row, column] = field[1, row, column] - modulus(x, y - 1) * u


def image_kernel(residual, unit_old, beside, layer_map, *refs):
    halos, (faces, k_rim_in, rim, field, product, unit, k_rim, q) = refs[:4], refs[4:]
    halos = surroundings(*halos)
    flow = lax.axis_index("group") == 0
    fill(residual, field, halos)

    @pl.when(flow)
    def _():
        hot = one_hot(layer_map)
        complete(faces, rim, k_rim_in, k_rim, halos, hot)
        parts = row_parts(faces, rim)

        def row(view, i, fx_before):
            out, fx = flow_row(view, field, i, fx_before)
            for k in range(3):
                product[k, i] = out[k]
            return fx

        run_rows(parts, 1, EX - 1, row, x_flux(parts[0], field, 0))
        unit[0] = gather_wide(field, hot)
        unit[1] = gather_wide(product, hot)

    @pl.when(jnp.logical_not(flow))
    def _():
        complete(faces, rim, k_rim_in, k_rim, halos, None)
        late_terms(faces, rim, field, beside, halos)
        unit_surroundings(unit_old, halos, q)
        load_rows([q], [field], True)
        solid_image(row_parts(faces, rim), [field], [product], 3)


def early_kernel(field, product, faces, state, sums, acc):
    flow = lax.axis_index("group") == 0

    @pl.when(flow)
    def _():
        def dots(i, acc):
            acc = list(acc)
            inside, last = tile_rows(), lanes(EY) == Z - 1

            def add(n, v):
                acc[n] = acc[n] + fold(jnp.where(inside, v, 0.0))

            ws = [product[k, i] for k in range(3)]
            below = flow_below(ws, last)
            g = m1 = m2 = m3 = cr = cw = 0.0
            for k in range(3):
                r, w = field[k, i], ws[k]
                dx, dy, dz = w - product[k, i + 1], w - up_y(w), w - below[k]
                cf = faces[9 + k, i]
                g = g + r * r
                m1 = m1 + r * w
                m2 = m2 + w * w
                cr = cr + cf * r
                cw = cw + cf * w
                m3 = m3 + (
                    faces[k, i] * dx * dx
                    + faces[3 + k, i] * dy * dy
                    + faces[6 + k, i] * dz * dz
                    + cf * w * w
                )
            for n, v in enumerate((g, m1, m2, m3, cr, cw)):
                add(n, v)
            weight = jnp.where(last, faces[8, i], 0.0)
            add(6, weight * field[2, i])
            add(7, weight * ws[2])
            acc[8] = acc[8] + fold(to_tile(weight) * state[2, i - OX])
            return tuple(acc)

        zero = jnp.zeros((8, Z), F32)
        found = dict(enumerate(loop(OX, OX + X, dots, (zero,) * FIRST_SUM, 2)))
        sums[...] = spread_sums(found)

    @pl.when(jnp.logical_not(flow))
    def _():
        sums[...] = spread_sums(gram_sums(faces, [field], [product], PAIRS[:1], acc))


def sums_kernel(field, product, faces, rim, unit, sums_in, sums, field12, product12, acc):
    flow = lax.axis_index("group") == 0
    everyone = sums.shape[0]

    @pl.when(flow)
    def _():
        sums[...] = jnp.broadcast_to(sums_in[:1], (everyone, Z))

    @pl.when(jnp.logical_not(flow))
    def _():
        fields = [field] + [field12.at[a] for a in range(2)]
        products = [product] + [product12.at[a] for a in range(2)]
        load_rows([unit.at[a] for a in range(2)], fields[1:], False)
        solid_image(row_parts(faces, rim), fields[1:], products[1:], 2)
        found = gram_sums(faces, fields, products, PAIRS[1:], acc)
        own = sums_in[:1] + spread_sums(found)[:1]
        sums[...] = jnp.broadcast_to(own, (everyone, Z))


def two_sum(a, b):
    s = a + b
    t = s - a
    return s, (a - (s - t)) + (b - t)


def quick(a, b):
    s = a + b
    return s, b - (s - a)


def halves(a):
    t = 4097.0 * a
    high = t - (t - a)
    return high, a - high


def two_product(a, b):
    p = a * b
    ah, al = halves(a)
    bh, bl = halves(b)
    return p, ((ah * bh - p) + ah * bl + al * bh) + al * bl


def pair_add(a, b):
    s, e = two_sum(a[0], b[0])
    return quick(s, e + (a[1] + b[1]))


def pair_less(a, b):
    return pair_add(a, (-b[0], -b[1]))


def pair_times(a, b):
    p, e = two_product(a[0], b[0])
    return quick(p, e + (a[0] * b[1] + a[1] * b[0]))


def pair_over(a, b):
    q = a[0] / b[0]
    rest = pair_less(a, pair_times(b, (q, jnp.zeros_like(q))))
    return quick(q, rest[0] / b[0])


def krylov(g, m1, m2, m3):
    a0 = pair_over(g, m1)
    h = pair_times(a0, pair_over(m2, m1))
    one = (jnp.ones_like(a0[0]), jnp.zeros_like(a0[0]))
    rho = pair_less(h, one)[0]
    third = pair_times(pair_times(a0, a0), pair_over(m3, m1))
    sigma = pair_less(third, pair_times(h, h))[0]
    more = (rho > 1e-9) & (sigma > 1e-9)
    a1 = jnp.where(more, a0[0] * rho / jnp.where(more, sigma, 1.0), 0.0)
    return a0[0] + a1 * h[0], -a0[0] * a1


def final_kernel(sums, state, field, product, field12, product12, out, balance, *, cells):
    flow = lax.axis_index("group") == 0
    total = (sums[...], jnp.zeros(sums.shape, F32))
    while total[0].shape[0] > 8:
        half = total[0].shape[0] // 2
        total = pair_add([v[:half] for v in total], [v[half:] for v in total])
    for step in (4, 2, 1):
        total = pair_add(total, [pltpu.roll(v, step, 0) for v in total])

    def number(n):
        return tuple(jnp.broadcast_to(v[:1, n : n + 1], (8, Z)) for v in total)

    c0, c1 = krylov(number(0), number(1), number(2), number(3))
    columns = cells // (3 * Z)
    outflow = (number(8)[0] + c0 * number(6)[0] + c1 * number(7)[0]) / columns
    stored = (c0 * number(4)[0] + c1 * number(5)[0]) / cells
    balance[0] = outflow[0, 0]
    balance[1] = stored[0, 0]

    def tall(v):
        return jnp.concatenate([v] * (EY // 8), axis=0)

    @pl.when(flow)
    def _():
        s0, s1 = tall(c0), tall(c1)

        def row(x, carry):
            for k in range(3):
                step = s0 * field[k, OX + x] + s1 * product[k, OX + x]
                out[k, x] = state[k, x] + to_tile(step)
            return carry

        loop(0, X, row)

    @pl.when(jnp.logical_not(flow))
    def _():
        zero = jnp.zeros((8, Z), F32)
        weights = [
            (jnp.ones((8, Z), F32), zero),
            (2.0 * c0, zero),
            (2.0 * c1, zero),
            two_product(c0, c0),
            two_product(2.0 * c0, c1),
            two_product(c1, c1),
        ]
        moments = []
        for m in range(4):
            start = FIRST_SUM + 6 * m
            total = number(start)
            for n in range(1, 6):
                total = pair_add(total, pair_times(weights[n], number(start + n)))
            moments.append(total)
        d0, d1 = krylov(*moments)
        scale_r = [tall(d0), tall(d0 * c0), tall(d0 * c1)]
        scale_w = [tall(d1), tall(d1 * c0), tall(d1 * c1)]

        def row(x, carry):
            for c in range(3):
                step = scale_r[0] * field[c, OX + x] + scale_w[0] * product[c, OX + x]
                for a in range(2):
                    step = step + scale_r[a + 1] * field12[a, c, OX + x]
                    step = step + scale_w[a + 1] * product12[a, c, OX + x]
                out[c, x] = state[c, x] + to_tile(step)
            return carry

        loop(0, X, row)


def swaps(first, second, axis):
    groups, rows, columns = (lax.axis_size(a) for a in AXES)
    count, found = lax.axis_size(axis), []
    for value, start in ((first, 0), (second, 1)):
        pairs = []
        for g in range(groups):
            for i in range(rows):
                for j in range(columns):
                    place = i if axis == "gx" else j
                    step = 1 if place % 2 == start else -1
                    if 0 <= place + step < count:
                        here = (g * rows + i) * columns + j
                        pairs.append((here, here + step * (columns if axis == "gx" else 1)))
        found.append(lax.ppermute(value, AXES, pairs))
    return found


def core_swap(value):
    count = lax.axis_size("gx") * lax.axis_size("gy")
    pairs = [(n, (n + count) % (2 * count)) for n in range(2 * count)]
    return lax.ppermute(value, AXES, pairs)


def body(state, conduct, capacity, supply, flags, layer_map):
    state, conduct, capacity, supply = state[0], conduct[0], capacity[0], supply[0]
    layer_map = layer_map.reshape(1, 3 * Z)
    cells = X * Y * 3 * Z * lax.axis_size("gx") * lax.axis_size("gy")
    devices = lax.axis_size("group") * lax.axis_size("gx") * lax.axis_size("gy")
    tile = struct(3, X, Y, Z)
    brick = struct(X, Y, Z)
    wide = (EX, EY, Z)
    full = struct(3, *wide)

    y_face = struct(len(Y_ROWS), X, Z)
    xa, xb, ya, yb = call(
        pack_kernel,
        x_faces(X_ROWS) + [y_face] * 2,
        [
            pltpu.VMEM((X, Y), jnp.int32),
            pltpu.VMEM((3, X, Y, Z), F32),
            pltpu.VMEM((3, 3, X, Y, Z), F32),
            pltpu.VMEM((X, Y, Z), F32),
            pltpu.VMEM((X, Y, Z), F32),
            pltpu.VMEM((3, X, Y, Z), F32),
            pltpu.SemaphoreType.DMA((14,)),
        ],
        left=(0, 1, 2, 3),
        limit=58,
        count=4,
    )(flags, state, conduct, capacity)
    k_halos = lax.optimization_barrier(swaps(xa, xb, "gx") + swaps(ya, yb, "gy"))
    wide_faces = struct(12, *wide)
    tables = [pltpu.VMEM((6, *wide), F32), pltpu.VMEM(wide, F32)]
    inner, tz, unit0 = call(
        interior_kernel,
        [wide_faces, tile, brick],
        tables + [pltpu.VMEM((X, Y, Z), F32)],
        cost=30_000_000,
    )(state, conduct, capacity, flags, layer_map)
    cross = core_swap(call(strain_kernel, brick)(state, unit0, *k_halos))
    base, beside = call(
        first_kernel,
        [tile, struct(8, Z)],
        tables + [pltpu.VMEM((3, *wide), F32)],
        cost=20_000_000,
    )(state, conduct, capacity, supply, inner, *k_halos)
    faces, k_rim = call(
        halo_kernel, [wide_faces, struct(6, len(K_RIM), EY, Z)], tables, cost=30_000_000
    )(conduct, capacity, tz, layer_map, *k_halos)
    residual, xa, xb = call(residual_kernel, [tile] + x_faces(R_ROWS))(
        base, cross, cross, layer_map
    )
    halos = swaps(xa, xb, "gx")
    ya, yb = call(relay_kernel, [struct(Y_PACK, Z)] * 2)(
        residual, cross, *halos, k_halos[0], k_halos[1]
    )
    halos = halos + swaps(ya, yb, "gy")
    rim, field, product, unit12 = call(
        image_kernel,
        [struct(12, len(RIM), EY, Z), full, full, struct(2, EX - 2, EY, Z)],
        [pltpu.VMEM((6, len(K_RIM), EY, Z), F32), pltpu.VMEM((EX - 2, EY, Z), F32)],
    )(residual, cross, beside, layer_map, *halos, faces, k_rim)
    unit12 = core_swap(unit12)
    sums = call(early_kernel, struct(8, Z), [pltpu.VMEM((4, 8, Z), F32)], cost=20_000_000)(
        field, product, faces, state
    )
    sums, field12, product12 = call(
        sums_kernel,
        [struct(devices, Z), struct(2, 3, *wide), struct(2, 3, *wide)],
        [pltpu.VMEM((20, 8, Z), F32)],
    )(field, product, faces, rim, unit12, sums)
    sums = lax.all_to_all(sums, AXES, 0, 0, tiled=True)

    def finish(*refs):
        final_kernel(*refs, cells=cells)

    new_state, balance = call(finish, [tile, struct(2)], scalars=(1,))(
        sums, state, field, product, field12, product12
    )
    return new_state[None], balance


def solution(mesh):
    placed = (
        P("group", None, "gx", "gy", None),
        P("group", None, None, "gx", "gy", None),
        P("group", "gx", "gy", None),
        P("group", None, "gx", "gy", None),
        P("gx", "gy"),
        P(),
    )
    return jax.shard_map(
        body,
        mesh=mesh,
        in_specs=placed,
        out_specs=(P("group", None, "gx", "gy", None), P()),
        check_vma=False,
    )
```

profile of v0, /device:TPU:1, one launch (start us, length us, event | category | flops | bytes accessed | tf_op | source)
XLA Modules:
  0.0 80.9 jit_solution(13360918522845492070)
XLA Ops:
  0.6 0.0 copy-start.4
  0.6 0.0 copy-start.2
  0.7 0.0 copy-start
  0.7 0.0 copy-start.1
  0.7 0.0 copy-start.5
  0.7 3.4 %shard_map.78 = (f32[26,32,128]{2,1,0:T(8,128)}, f32[26,32,128]{2,1,0:T(8,128)}, f32[26,16,128]{2,1,0:T(8,128)}, f32[26,16,128]{2,1,0:T(8,128)}) custom-call(s32[16,32]{1,0:T(8,128)} %flags_in.1, f32[3,16,32,128]{3,2,1,0:T(8,128)} %bitcast.13, f32[3,3,16,32,128]{4,3,2,1,0:T(8,128)} %bitcast.9, f32[16,32,128]{2,1,0:T(8,128)} %bitcast.19), custom_call_target="tpu_custom_call" | custom-call | tf_op jit(solution)/shard_map/pallas_call | solution.py:1044
  4.0 2.1 %collective-permute-start = (f32[26,32,128]{2,1,0:T(8,128)}, f32[26,32,128]{2,1,0:T(8,128)S(1)}, u32[]{:S(2)}, u32[]{:S(2)}) collective-permute-start(f32[26,32,128]{2,1,0:T(8,128)} %get-tuple-element.32), channel_id=1, source_target_pairs={{0,8},{1,9},{2,10},{3,11},{4,12},{5,13},{6,14},{7,15},{8,0},{9,1},... | collective-permute-start | bytes 1277960 | tf_op jit(solution)/shard_map/ppermute | solution.py:1023
  6.2 0.7 collective-permute-start.1
  6.9 1.4 %collective-permute-start.2 = (f32[26,16,128]{2,1,0:T(8,128)}, f32[26,16,128]{2,1,0:T(8,128)S(1)}, u32[]{:S(2)}, u32[]{:S(2)}) collective-permute-start(f32[26,16,128]{2,1,0:T(8,128)} %get-tuple-element.34), channel_id=1, source_target_pairs={{0,1},{1,0},{2,3},{3,2},{4,5},{5,4},{6,7},{7,6},{8,9},{9,8},{10,11... | collective-permute-start | bytes 638984 | tf_op jit(solution)/shard_map/ppermute | solution.py:1023
  8.2 0.7 collective-permute-start.3
  8.9 0.0 copy-done.5
  8.9 0.0 copy-done.4
  8.9 0.0 copy-done.2
  8.9 0.0 copy-done
  9.0 0.0 copy-done.1
  9.0 0.0 copy-start.3
  9.0 1.4 %shard_map.77 = (f32[12,22,40,128]{3,2,1,0:T(8,128)S(1)}, f32[3,16,32,128]{3,2,1,0:T(8,128)S(1)}, f32[16,32,128]{2,1,0:T(8,128)S(1)}) custom-call(f32[3,16,32,128]{3,2,1,0:T(8,128)S(1)} %bitcast.14, f32[3,3,16,32,128]{4,3,2,1,0:T(8,128)S(1)} %bitcast.10, f32[16,32,128]{2,1,0:T(8,128)S(1)} %bitcast.20, s32[16,32]{1,0:T(8,128)S(1)} %copy-done.4, ...), custom_call_target="tpu_custom_call" | custom-call | flops 30000000 | bytes 30000000 | tf_op jit(solution)/shard_map/pallas_call | solution.py:1063
  10.4 2.5 %collective-permute-done.2.ya = f32[26,16,128]{2,1,0:T(8,128)S(1)} collective-permute-done((f32[26,16,128]{2,1,0:T(8,128)}, f32[26,16,128]{2,1,0:T(8,128)S(1)}, u32[]{:S(2)}, u32[]{:S(2)}) %collective-permute-start.2) | collective-permute-done | bytes 213024 | tf_op jit(solution)/shard_map/ppermute | solution.py:1023
  12.9 0.0 collective-permute-done.3.yb
  12.9 2.5 %collective-permute-done.xa.ka = f32[26,32,128]{2,1,0:T(8,128)S(1)} collective-permute-done((f32[26,32,128]{2,1,0:T(8,128)}, f32[26,32,128]{2,1,0:T(8,128)S(1)}, u32[]{:S(2)}, u32[]{:S(2)}) %collective-permute-start) | collective-permute-done | bytes 426016 | tf_op jit(solution)/shard_map/ppermute | solution.py:1023
  15.4 0.0 collective-permute-done.1.xb.kb
  15.4 0.1 shard_map.80
  15.6 1.7 %collective-permute-start.4 = (f32[16,32,128]{2,1,0:T(8,128)S(1)}, f32[16,32,128]{2,1,0:T(8,128)S(1)}, u32[]{:S(2)}, u32[]{:S(2)}) collective-permute-start(f32[16,32,128]{2,1,0:T(8,128)S(1)} %shard_map.80), channel_id=1, source_target_pairs={{0,64},{1,65},{2,66},{3,67},{4,68},{5,69},{6,70},{7,71},{8,72},{9,... | collective-permute-start | bytes 786440 | tf_op jit(solution)/shard_map/ppermute | solution.py:1030
  17.3 0.0 copy-done.3
  17.3 1.7 %shard_map.79 = (f32[3,16,32,128]{3,2,1,0:T(8,128)S(1)}, f32[8,128]{1,0:T(8,128)S(1)}) custom-call(f32[3,16,32,128]{3,2,1,0:T(8,128)S(1)} %bitcast.16, f32[3,3,16,32,128]{4,3,2,1,0:T(8,128)S(1)} %bitcast.11, f32[16,32,128]{2,1,0:T(8,128)S(1)} %bitcast.21, f32[3,16,32,128]{3,2,1,0:T(8,128)S(1)} %bitcast.23, ...), custom_call_target="tpu_custom_call" | custom-call | flops 20000000 | bytes 20000000 | tf_op jit(solution)/shard_map/pallas_call | solution.py:1070
  19.0 0.0 collective-permute-done.4.strain.unit.unit_old
  19.0 0.1 shard_map.81
  19.1 4.1 %collective-permute-start.5 = (f32[9,32,128]{2,1,0:T(8,128)S(1)}, f32[9,32,128]{2,1,0:T(8,128)S(1)}, u32[]{:S(2)}, u32[]{:S(2)}) collective-permute-start(f32[9,32,128]{2,1,0:T(8,128)S(1)} %get-tuple-element.44), channel_id=1, source_target_pairs={{0,8},{1,9},{2,10},{3,11},{4,12},{5,13},{6,14},{7,15},{8,0},{9,1},... | collective-permute-start | bytes 442376 | tf_op jit(solution)/shard_map/ppermute | solution.py:1023
  23.2 0.7 collective-permute-start.6
  23.9 3.5 %collective-permute-done.5.xa.refs_0_ = f32[9,32,128]{2,1,0:T(8,128)S(1)} collective-permute-done((f32[9,32,128]{2,1,0:T(8,128)S(1)}, f32[9,32,128]{2,1,0:T(8,128)S(1)}, u32[]{:S(2)}, u32[]{:S(2)}) %collective-permute-start.5) | collective-permute-done | bytes 147488 | tf_op jit(solution)/shard_map/ppermute | solution.py:1023
  27.3 0.0 collective-permute-done.6.xb.refs_1_
  27.3 0.3 shard_map.82
  27.6 1.4 %collective-permute-start.7 = (f32[280,128]{1,0:T(8,128)S(1)}, f32[280,128]{1,0:T(8,128)S(1)}, u32[]{:S(2)}, u32[]{:S(2)}) collective-permute-start(f32[280,128]{1,0:T(8,128)S(1)} %get-tuple-element.46), channel_id=1, source_target_pairs={{0,1},{1,0},{2,3},{3,2},{4,5},{5,4},{6,7},{7,6},{8,9},{9,8},{10,11... | collective-permute-start | bytes 430088 | tf_op jit(solution)/shard_map/ppermute | solution.py:1023
  29.0 0.7 collective-permute-start.8
  29.7 1.2 %shard_map.83 = (f32[12,22,40,128]{3,2,1,0:T(8,128)S(1)}, f32[6,8,40,128]{3,2,1,0:T(8,128)S(1)}) custom-call(f32[3,3,16,32,128]{4,3,2,1,0:T(8,128)S(1)} %bitcast.12, f32[16,32,128]{2,1,0:T(8,128)S(1)} %bitcast.22, f32[3,16,32,128]{3,2,1,0:T(8,128)S(1)} %get-tuple-element.48.tz, s32[1,384]{1,0:T(1,128)S(1)} %reshape.9.layer_map, ...), custom_call_target="tpu_custom_call" | custom-call | flops 30000000 | bytes 30000000 | tf_op jit(solution)/shard_map/pallas_call | solution.py:1076
  30.8 1.5 %collective-permute-done.7.refs_2_ = f32[280,128]{1,0:T(8,128)S(1)} collective-permute-done((f32[280,128]{1,0:T(8,128)S(1)}, f32[280,128]{1,0:T(8,128)S(1)}, u32[]{:S(2)}, u32[]{:S(2)}) %collective-permute-start.7) | collective-permute-done | bytes 143392 | tf_op jit(solution)/shard_map/ppermute | solution.py:1023
  32.3 0.0 collective-permute-done.8.refs_3_
  32.3 2.4 %shard_map.84 = (f32[12,6,40,128]{3,2,1,0:T(8,128)S(1)}, f32[3,22,40,128]{3,2,1,0:T(8,128)S(1)}, f32[3,22,40,128]{3,2,1,0:T(8,128)S(1)}, f32[2,20,40,128]{3,2,1,0:T(8,128)S(1)}) custom-call(f32[3,16,32,128]{3,2,1,0:T(8,128)S(1)} %get-tuple-element.42.residual, f32[16,32,128]{2,1,0:T(8,128)S(1)} %collective-permute-done.4.strain.unit.unit_old, ...), custom_call_target="tpu_custom_call" | custom-call | tf_op jit(solution)/shard_map/pallas_call | solution.py:1087
  34.8 1.8 %collective-permute-start.9 = (f32[2,20,40,128]{3,2,1,0:T(8,128)S(1)}, f32[2,20,40,128]{3,2,1,0:T(8,128)S(1)}, u32[]{:S(2)}, u32[]{:S(2)}) collective-permute-start(f32[2,20,40,128]{3,2,1,0:T(8,128)S(1)} %get-tuple-element.54), channel_id=1, source_target_pairs={{0,64},{1,65},{2,66},{3,67},{4,68},{5,69},{6,70},{7,71},{8,72},{9,... | collective-permute-start | bytes 2457608 | tf_op jit(solution)/shard_map/ppermute | solution.py:1030
  36.6 1.1 %shard_map.85.sums_in = f32[8,128]{1,0:T(8,128)S(1)} custom-call(f32[3,22,40,128]{3,2,1,0:T(8,128)S(1)} %get-tuple-element.51.field.refs_2_, f32[3,22,40,128]{3,2,1,0:T(8,128)S(1)} %get-tuple-element.52.product.refs_3_, f32[12,22,40,128]{3,2,1,0:T(8,128)S(1)} %get-tuple-element.49.refs_4_.faces, f32[3,16,32,128]{3,2,1,0:T(8,128)S(1)} %bitcast.17), custom_call_target="tpu_custom_call" | custom-call | flops 20000000 | bytes 20000000 | tf_op jit(solution)/shard_map/pallas_call | solution.py:1093
  37.7 0.8 %collective-permute-done.9.unit = f32[2,20,40,128]{3,2,1,0:T(8,128)S(1)} collective-permute-done((f32[2,20,40,128]{3,2,1,0:T(8,128)S(1)}, f32[2,20,40,128]{3,2,1,0:T(8,128)S(1)}, u32[]{:S(2)}, u32[]{:S(2)}) %collective-permute-start.9) | collective-permute-done | bytes 819232 | tf_op jit(solution)/shard_map/ppermute | solution.py:1030
  38.6 7.4 %shard_map.86 = (f32[128,128]{1,0:T(8,128)S(1)}, f32[2,3,22,40,128]{4,3,2,1,0:T(8,128)S(1)}, f32[2,3,22,40,128]{4,3,2,1,0:T(8,128)S(1)}) custom-call(f32[3,22,40,128]{3,2,1,0:T(8,128)S(1)} %get-tuple-element.51.field.refs_2_, f32[3,22,40,128]{3,2,1,0:T(8,128)S(1)} %get-tuple-element.52.product.refs_3_, ...), custom_call_target="tpu_custom_call" | custom-call | tf_op jit(solution)/shard_map/pallas_call | solution.py:1096
  46.0 33.0 %all_to_all.11 = f32[128,1,128]{2,1,0:T(1,128)S(1)} all-to-all(f32[128,1,128]{2,1,0:T(1,128)S(1)} %bitcast.25), channel_id=1, replica_groups=mesh['group'=2,'gx'=8,'gy'=8] {'group','gx','gy'}, dimensions={0} | all-to-all | bytes 131072 | tf_op jit(solution)/shard_map/all_to_all | solution.py:1101
  78.9 1.9 %shard_map.87 = (f32[3,16,32,128]{3,2,1,0:T(8,128)}, f32[2]{0:T(128)}) custom-call(f32[128,128]{1,0:T(8,128)S(1)} %bitcast.24, f32[3,16,32,128]{3,2,1,0:T(8,128)S(1)} %bitcast.18, f32[3,22,40,128]{3,2,1,0:T(8,128)S(1)} %get-tuple-element.51.field.refs_2_, f32[3,22,40,128]{3,2,1,0:T(8,128)S(1)} %get-tuple-element.52.product.refs_3_, ...), custom_call_target="tpu_custom_call" | custom-call | tf_op jit(solution)/shard_map/pallas_call | solution.py:1106
  (1 shorter events, 0.0 us)
Async XLA Ops:
  0.6 8.3 %copy-start.4 = (s32[16,32]{1,0:T(8,128)S(1)}, s32[16,32]{1,0:T(8,128)}, u32[]{:S(2)}) copy-start(s32[16,32]{1,0:T(8,128)} %flags_in.1) | copy-start | bytes 6148
  0.6 8.3 %copy-start.2 = (f32[1,16,32,128]{3,2,1,0:T(8,128)S(1)}, f32[1,16,32,128]{3,2,1,0:T(8,128)}, u32[]{:S(2)}) copy-start(f32[1,16,32,128]{3,2,1,0:T(8,128)} %param.8) | copy-start | bytes 786436
  0.7 8.3 %copy-start = (f32[1,3,3,16,32,128]{5,4,3,2,1,0:T(8,128)S(1)}, f32[1,3,3,16,32,128]{5,4,3,2,1,0:T(8,128)}, u32[]{:S(2)}) copy-start(f32[1,3,3,16,32,128]{5,4,3,2,1,0:T(8,128)} %param.7) | copy-start | bytes 7077892
  0.7 8.3 %copy-start.1 = (f32[1,3,16,32,128]{4,3,2,1,0:T(8,128)S(1)}, f32[1,3,16,32,128]{4,3,2,1,0:T(8,128)}, u32[]{:S(2)}) copy-start(f32[1,3,16,32,128]{4,3,2,1,0:T(8,128)} %param.6) | copy-start | bytes 2359300
  0.7 8.2 %copy-start.5 = (s32[384]{0:T(512)S(1)}, s32[384]{0:T(512)}, u32[]{:S(2)}) copy-start(s32[384]{0:T(512)} %param.11) | copy-start | bytes 4612
  4.0 11.4 %collective-permute-start = (f32[26,32,128]{2,1,0:T(8,128)}, f32[26,32,128]{2,1,0:T(8,128)S(1)}, u32[]{:S(2)}, u32[]{:S(2)}) collective-permute-start(f32[26,32,128]{2,1,0:T(8,128)} %get-tuple-element.32), channel_id=1, source_target_pairs={{0,8},{1,9},{2,10},{3,11},{4,12},{5,13},{6,14},{7,15},{8,0},{9,1},... | collective-permute-start | bytes 1277960 | tf_op jit(solution)/shard_map/ppermute | solution.py:1023
  6.2 9.2 %collective-permute-start.1 = (f32[26,32,128]{2,1,0:T(8,128)}, f32[26,32,128]{2,1,0:T(8,128)S(1)}, u32[]{:S(2)}, u32[]{:S(2)}) collective-permute-start(f32[26,32,128]{2,1,0:T(8,128)} %get-tuple-element.33), channel_id=1, source_target_pairs={{8,16},{9,17},{10,18},{11,19},{12,20},{13,21},{14,22},{15,23},{16,... | collective-permute-start | bytes 1277960 | tf_op jit(solution)/shard_map/ppermute | solution.py:1023
  6.9 6.1 %collective-permute-start.2 = (f32[26,16,128]{2,1,0:T(8,128)}, f32[26,16,128]{2,1,0:T(8,128)S(1)}, u32[]{:S(2)}, u32[]{:S(2)}) collective-permute-start(f32[26,16,128]{2,1,0:T(8,128)} %get-tuple-element.34), channel_id=1, source_target_pairs={{0,1},{1,0},{2,3},{3,2},{4,5},{5,4},{6,7},{7,6},{8,9},{9,8},{10,11... | collective-permute-start | bytes 638984 | tf_op jit(solution)/shard_map/ppermute | solution.py:1023
  8.2 4.7 %collective-permute-start.3 = (f32[26,16,128]{2,1,0:T(8,128)}, f32[26,16,128]{2,1,0:T(8,128)S(1)}, u32[]{:S(2)}, u32[]{:S(2)}) collective-permute-start(f32[26,16,128]{2,1,0:T(8,128)} %get-tuple-element.35), channel_id=1, source_target_pairs={{1,2},{2,1},{3,4},{4,3},{5,6},{6,5},{9,10},{10,9},{11,12},{12,11},... | collective-permute-start | bytes 638984 | tf_op jit(solution)/shard_map/ppermute | solution.py:1023
  9.0 8.3 %copy-start.3 = (f32[1,3,16,32,128]{4,3,2,1,0:T(8,128)S(1)}, f32[1,3,16,32,128]{4,3,2,1,0:T(8,128)}, u32[]{:S(2)}) copy-start(f32[1,3,16,32,128]{4,3,2,1,0:T(8,128)} %param.9) | copy-start | bytes 2359300
  15.6 3.4 %collective-permute-start.4 = (f32[16,32,128]{2,1,0:T(8,128)S(1)}, f32[16,32,128]{2,1,0:T(8,128)S(1)}, u32[]{:S(2)}, u32[]{:S(2)}) collective-permute-start(f32[16,32,128]{2,1,0:T(8,128)S(1)} %shard_map.80), channel_id=1, source_target_pairs={{0,64},{1,65},{2,66},{3,67},{4,68},{5,69},{6,70},{7,71},{8,72},{9,... | collective-permute-start | bytes 786440 | tf_op jit(solution)/shard_map/ppermute | solution.py:1030
  19.1 8.2 %collective-permute-start.5 = (f32[9,32,128]{2,1,0:T(8,128)S(1)}, f32[9,32,128]{2,1,0:T(8,128)S(1)}, u32[]{:S(2)}, u32[]{:S(2)}) collective-permute-start(f32[9,32,128]{2,1,0:T(8,128)S(1)} %get-tuple-element.44), channel_id=1, source_target_pairs={{0,8},{1,9},{2,10},{3,11},{4,12},{5,13},{6,14},{7,15},{8,0},{9,1},... | collective-permute-start | bytes 442376 | tf_op jit(solution)/shard_map/ppermute | solution.py:1023
  23.2 4.1 %collective-permute-start.6 = (f32[9,32,128]{2,1,0:T(8,128)S(1)}, f32[9,32,128]{2,1,0:T(8,128)S(1)}, u32[]{:S(2)}, u32[]{:S(2)}) collective-permute-start(f32[9,32,128]{2,1,0:T(8,128)S(1)} %get-tuple-element.45), channel_id=1, source_target_pairs={{8,16},{9,17},{10,18},{11,19},{12,20},{13,21},{14,22},{15,23},{16,... | collective-permute-start | bytes 442376 | tf_op jit(solution)/shard_map/ppermute | solution.py:1023
  27.6 4.7 %collective-permute-start.7 = (f32[280,128]{1,0:T(8,128)S(1)}, f32[280,128]{1,0:T(8,128)S(1)}, u32[]{:S(2)}, u32[]{:S(2)}) collective-permute-start(f32[280,128]{1,0:T(8,128)S(1)} %get-tuple-element.46), channel_id=1, source_target_pairs={{0,1},{1,0},{2,3},{3,2},{4,5},{5,4},{6,7},{7,6},{8,9},{9,8},{10,11... | collective-permute-start | bytes 430088 | tf_op jit(solution)/shard_map/ppermute | solution.py:1023
  29.0 3.3 %collective-permute-start.8 = (f32[280,128]{1,0:T(8,128)S(1)}, f32[280,128]{1,0:T(8,128)S(1)}, u32[]{:S(2)}, u32[]{:S(2)}) collective-permute-start(f32[280,128]{1,0:T(8,128)S(1)} %get-tuple-element.47), channel_id=1, source_target_pairs={{1,2},{2,1},{3,4},{4,3},{5,6},{6,5},{9,10},{10,9},{11,12},{12,11},... | collective-permute-start | bytes 430088 | tf_op jit(solution)/shard_map/ppermute | solution.py:1023
  34.8 3.8 %collective-permute-start.9 = (f32[2,20,40,128]{3,2,1,0:T(8,128)S(1)}, f32[2,20,40,128]{3,2,1,0:T(8,128)S(1)}, u32[]{:S(2)}, u32[]{:S(2)}) collective-permute-start(f32[2,20,40,128]{3,2,1,0:T(8,128)S(1)} %get-tuple-element.54), channel_id=1, source_target_pairs={{0,64},{1,65},{2,66},{3,67},{4,68},{5,69},{6,70},{7,71},{8,72},{9,... | collective-permute-start | bytes 2457608 | tf_op jit(solution)/shard_map/ppermute | solution.py:1030
where the time goes:
time: 81.1 us; the launch traced here: 80.9 us
  blocking collectives  33 us (41%)
  Pallas kernels  21 us (26%)
  starting transfers between devices  15.2 us (19%)
  waiting for transfers between devices  10.8 us (13%)
  between operations  0.85 us (1%)
    all_to_all x1, blocking collectives, body(): sums = lax.all_to_all(sums, AXES, 0, 0, tiled=True)  33 us
    ppermute x8, starting transfers between devices, swaps(): found.append(lax.ppermute(value, AXES, pairs))  11.6 us
    ppermute x8, waiting for transfers between devices, swaps(): found.append(lax.ppermute(value, AXES, pairs))  9.97 us
    pallas_call x1, Pallas kernels, body(): call(sums_kernel, [struct(devices, Z), struct(2, 3, *wide), struct(2, 3,...  7.39 us
    ppermute x2, starting transfers between devices, core_swap(): return lax.ppermute(value, AXES, pairs)  3.55 us
    pallas_call x1, Pallas kernels, body(): call(pack_kernel, x_faces(X_ROWS) + [y_face] * 2, [pltpu.VMEM((X, Y), jnp...  3.36 us
    pallas_call x1, Pallas kernels, body(): call(image_kernel, [struct(12, len(RIM), EY, Z), full, full, struct(2, EX...  2.42 us
    pallas_call x1, Pallas kernels, body(): call(finish, [tile, struct(2)], scalars=(1,))  1.93 us
  transfers between devices with their start and end apart: 10, of which 5 were waited for; matrix products, arithmetic and copies ran while one was open for 0% of the time, Pallas kernels for 7%

commit v1 on v0

--- a/solution.py
+++ b/solution.py
@@ -14,6 +14,8 @@
 F32 = jnp.float32
 
 X_ROWS = [(f, r) for f in range(13) for r in range(1, (3 if f < 3 else 2 if f < 10 else 1) + 1)]
+NEAR = [(f, r) for f, r in X_ROWS if r == 1 and not 3 <= f < 9]
+X_ROWS = NEAR + [row for row in X_ROWS if row not in NEAR]
 Y_ROWS = [
     (f, r) for f in range(13) for r in range(1, (3 if 3 <= f < 6 else 2 if f < 10 else 1) + 1)
 ]
@@ -134,6 +136,24 @@
     return copies
 
 
+class Joined:
+    def __init__(self, near, far):
+        self.near, self.far = near, far
+
+    def place(self, at):
+        n, rest = (at[0], at[1:]) if isinstance(at, tuple) else (at, ())
+        ref, n = (self.near, n) if n < len(NEAR) else (self.far, n - len(NEAR))
+        return ref, (n, *rest)
+
+    def __getitem__(self, at):
+        ref, at = self.place(at)
+        return ref[at]
+
+    def __setitem__(self, at, value):
+        ref, at = self.place(at)
+        ref[at] = value
+
+
 class Either:
     def __init__(self, odd, at_odd, at_even):
         self.odd, self.at_odd, self.at_even = odd, at_odd, at_even
@@ -225,7 +245,7 @@
     loop(0, X, row)
 
 
-def pack_kernel(flags_in, state_in, conduct_in, capacity_in, xa, xb, ya, yb, *scratch):
+def pack_kernel(flags_in, state_in, conduct_in, capacity_in, xa, xb, fa, fb, ya, yb, *scratch):
     flags, state, conduct, capacity, bottom, tz, sem = scratch
     early = [(flags_in, flags)] + [(conduct_in.at[2, k], conduct.at[2, k]) for k in range(3)]
     late = [(conduct_in.at[d, k], conduct.at[d, k]) for d in range(2) for k in range(3)]
@@ -248,7 +268,7 @@
             return tz.at[f - 6]
         return capacity if f == 9 else state.at[f - 10]
 
-    pack_x(source, X_ROWS, xa, xb)
+    pack_x(source, X_ROWS, Joined(xa, fa), Joined(xb, fb))
     odd = parity("gy")
     for n, (f, r) in enumerate(Y_ROWS):
         put(ya, yb, n, odd, source(f)[:, Y - r, :], source(f)[:, r - 1, :])
@@ -452,8 +472,9 @@
         loop(OX, OX + X, row, (before, x_flux(faces, field, OX - 1)))
 
 
-def halo_kernel(conduct, capacity, tz, layer_map, xa, xb, ya, yb, faces, rim, keep, caps):
-    xl, xu, yl, yu = surroundings(xa, xb, ya, yb)
+def halo_kernel(conduct, capacity, tz, layer_map, xa, xb, ya, yb, fa, fb, *refs):
+    faces, rim, keep, caps = refs
+    xl, xu, yl, yu = surroundings(Joined(xa, fa), Joined(xb, fb), ya, yb)
     flow = lax.axis_index("group") == 0
 
     def target(f):
@@ -523,10 +544,10 @@
             put(xa, xb, n, odd, unit[X - 1 - depth], unit[depth])
 
 
-def relay_kernel(residual, unit, xa, xb, ka, kb, ya, yb):
+def relay_kernel(residual, unit, xa, xb, ka, kb, fa, fb, ya, yb):
     flow = lax.axis_index("group") == 0
     odd = parity("gy")
-    r_halos, k_halos = lower_upper("gx", xa, xb), lower_upper("gx", ka, kb)
+    r_halos, k_halos = lower_upper("gx", xa, xb), lower_upper("gx", Joined(ka, fa), Joined(kb, fb))
 
     def give(at, count, ref, index, j):
         put(ya, yb, slice(at, at + count), odd, ref[index(Y - j)], ref[index(j - 1)])
@@ -1041,9 +1062,9 @@
     full = struct(3, *wide)
 
     y_face = struct(len(Y_ROWS), X, Z)
-    xa, xb, ya, yb = call(
+    xa, xb, fa, fb, ya, yb = call(
         pack_kernel,
-        x_faces(X_ROWS) + [y_face] * 2,
+        x_faces(NEAR) + x_faces(X_ROWS[len(NEAR) :]) + [y_face] * 2,
         [
             pltpu.VMEM((X, Y), jnp.int32),
             pltpu.VMEM((3, X, Y, Z), F32),
@@ -1058,6 +1079,7 @@
         count=4,
     )(flags, state, conduct, capacity)
     k_halos = lax.optimization_barrier(swaps(xa, xb, "gx") + swaps(ya, yb, "gy"))
+    far = swaps(fa, fb, "gx")
     wide_faces = struct(12, *wide)
     tables = [pltpu.VMEM((6, *wide), F32), pltpu.VMEM(wide, F32)]
     inner, tz, unit0 = call(
@@ -1075,13 +1097,13 @@
     )(state, conduct, capacity, supply, inner, *k_halos)
     faces, k_rim = call(
         halo_kernel, [wide_faces, struct(6, len(K_RIM), EY, Z)], tables, cost=30_000_000
-    )(conduct, capacity, tz, layer_map, *k_halos)
+    )(conduct, capacity, tz, layer_map, *k_halos, *far)
     residual, xa, xb = call(residual_kernel, [tile] + x_faces(R_ROWS))(
         base, cross, cross, layer_map
     )
     halos = swaps(xa, xb, "gx")
     ya, yb = call(relay_kernel, [struct(Y_PACK, Z)] * 2)(
-        residual, cross, *halos, k_halos[0], k_halos[1]
+        residual, cross, *halos, k_halos[0], k_halos[1], *far
     )
     halos = halos + swaps(ya, yb, "gy")
     rim, field, product, unit12 = call(

time: 81.1 us -> 80.9 us (level)
  starting transfers between devices: 15.2 us -> 24.5 us
  waiting for transfers between devices: 10.8 us -> 5.04 us
  blocking collectives: 33 us -> 29.2 us
    ppermute x8 -> x10, starting transfers between devices: 11.6 us -> 20.2 us  [swaps(): found.append(lax.ppermute(value, AXES, pairs))]
    ppermute x8 -> x10, waiting for transfers between devices: 9.97 us -> 4.2 us  [swaps(): found.append(lax.ppermute(value, AXES, pairs))]
    all_to_all x1, blocking collectives: 33 us -> 29.2 us  [body(): sums = lax.all_to_all(sums, AXES, 0, 0, tiled=True)]
  transfers between devices with their start and end apart: 10 -> 12, of which waited for: 5 -> 4; matrix products, arithmetic and copies ran while one was open for 0% -> 0% of each run, Pallas kernels for 7% -> 7%
where the time goes in v1:
time: 80.9 us; the launch traced here: 80.7 us
  blocking collectives  29.2 us (36%)
  starting transfers between devices  24.5 us (30%)
  Pallas kernels  21.1 us (26%)
  waiting for transfers between devices  5.04 us (6%)
  between operations  0.9 us (1%)
    all_to_all x1, blocking collectives, body(): sums = lax.all_to_all(sums, AXES, 0, 0, tiled=True)  29.2 us
    ppermute x10, starting transfers between devices, swaps(): found.append(lax.ppermute(value, AXES, pairs))  20.2 us
    pallas_call x1, Pallas kernels, body(): call(sums_kernel, [struct(devices, Z), struct(2, 3, *wide), struct(2, 3,...  7.38 us
    ppermute x2, starting transfers between devices, core_swap(): return lax.ppermute(value, AXES, pairs)  4.3 us
    ppermute x10, waiting for transfers between devices, swaps(): found.append(lax.ppermute(value, AXES, pairs))  4.2 us
    pallas_call x1, Pallas kernels, body(): call(pack_kernel, x_faces(NEAR) + x_faces(X_ROWS[len(NEAR):]) + [y_face]...  3.34 us
    pallas_call x1, Pallas kernels, body(): call(image_kernel, [struct(12, len(RIM), EY, Z), full, full, struct(2, EX...  2.42 us
    pallas_call x1, Pallas kernels, body(): call(finish, [tile, struct(2)], scalars=(1,))  1.93 us
  transfers between devices with their start and end apart: 12, of which 4 were waited for; matrix products, arithmetic and copies ran while one was open for 0% of the time, Pallas kernels for 7%

profile of v1, /device:TPU:1, one launch (start us, length us, event | category | flops | bytes accessed | tf_op | source)
XLA Modules:
  0.0 80.7 jit_solution(3616093979327180121)
XLA Ops:
  0.6 0.0 copy-start.4
  0.6 0.0 copy-start.2
  0.7 0.0 copy-start
  0.7 0.0 copy-start.1
  0.7 0.0 copy-start.5
  0.7 3.3 %shard_map.78 = (f32[7,32,128]{2,1,0:T(8,128)}, f32[7,32,128]{2,1,0:T(8,128)}, f32[19,32,128]{2,1,0:T(8,128)}, f32[19,32,128]{2,1,0:T(8,128)}, f32[26,16,128]{2,1,0:T(8,128)}, /*index=5*/f32[26,16,128]{2,1,0:T(8,128)}) custom-call(s32[16,32]{1,0:T(8,128)} %flags_in.1, f32[3,16,32,128]{3,2,1,0:T(8,128)} %bitcast.13, f32[3,3,16,32,128]{4,3,2,1,0:T(8,128)} %bitcast.9, ...), custom_call_target="tpu_custom_call" | custom-call | tf_op jit(solution)/shard_map/pallas_call | solution.py:1065
  4.0 0.0 copy-start.7
  4.0 0.0 copy-start.6
  4.0 0.0 copy-start.3
  4.1 2.2 %collective-permute-start.2 = (f32[26,16,128]{2,1,0:T(8,128)}, f32[26,16,128]{2,1,0:T(8,128)S(1)}, u32[]{:S(2)}, u32[]{:S(2)}) collective-permute-start(f32[26,16,128]{2,1,0:T(8,128)} %get-tuple-element.36), channel_id=1, source_target_pairs={{0,1},{1,0},{2,3},{3,2},{4,5},{5,4},{6,7},{7,6},{8,9},{9,8},{10,11... | collective-permute-start | bytes 638984 | tf_op jit(solution)/shard_map/ppermute | solution.py:1044
  6.3 0.7 collective-permute-start.3
  6.9 1.3 %collective-permute-start = (f32[7,32,128]{2,1,0:T(8,128)}, f32[7,32,128]{2,1,0:T(8,128)S(1)}, u32[]{:S(2)}, u32[]{:S(2)}) collective-permute-start(f32[7,32,128]{2,1,0:T(8,128)} %get-tuple-element.34), channel_id=1, source_target_pairs={{0,8},{1,9},{2,10},{3,11},{4,12},{5,13},{6,14},{7,15},{8,0},{9,1},... | collective-permute-start | bytes 344072 | tf_op jit(solution)/shard_map/ppermute | solution.py:1044
  8.2 0.7 collective-permute-start.1
  8.9 0.0 copy-done.5
  8.9 0.0 copy-done.4
  8.9 0.0 copy-done.2
  8.9 0.0 copy-done
  8.9 0.0 copy-done.1
  9.0 1.4 %shard_map.77 = (f32[12,22,40,128]{3,2,1,0:T(8,128)S(1)}, f32[3,16,32,128]{3,2,1,0:T(8,128)S(1)}, f32[16,32,128]{2,1,0:T(8,128)S(1)}) custom-call(f32[3,16,32,128]{3,2,1,0:T(8,128)S(1)} %bitcast.14, f32[3,3,16,32,128]{4,3,2,1,0:T(8,128)S(1)} %bitcast.10, f32[16,32,128]{2,1,0:T(8,128)S(1)} %bitcast.20, s32[16,32]{1,0:T(8,128)S(1)} %copy-done.4, ...), custom_call_target="tpu_custom_call" | custom-call | flops 30000000 | bytes 30000000 | tf_op jit(solution)/shard_map/pallas_call | solution.py:1085
  10.4 0.8 collective-permute-done.xa.ka
  11.2 0.0 collective-permute-done.1.xb.kb
  11.2 0.0 collective-permute-done.2.ya
  11.2 0.0 collective-permute-done.3.yb
  11.2 0.2 shard_map.80
  11.3 1.8 %collective-permute-start.4 = (f32[16,32,128]{2,1,0:T(8,128)S(1)}, f32[16,32,128]{2,1,0:T(8,128)S(1)}, u32[]{:S(2)}, u32[]{:S(2)}) collective-permute-start(f32[16,32,128]{2,1,0:T(8,128)S(1)} %shard_map.80), channel_id=1, source_target_pairs={{0,64},{1,65},{2,66},{3,67},{4,68},{5,69},{6,70},{7,71},{8,72},{9,... | collective-permute-start | bytes 786440 | tf_op jit(solution)/shard_map/ppermute | solution.py:1051
  13.1 0.0 copy-done.7
  13.1 3.8 %collective-permute-start.7 = (f32[19,32,128]{2,1,0:T(8,128)S(1)}, f32[19,32,128]{2,1,0:T(8,128)S(1)}, u32[]{:S(2)}, u32[]{:S(2)}) collective-permute-start(f32[19,32,128]{2,1,0:T(8,128)S(1)} %copy-done.7), channel_id=1, source_target_pairs={{0,8},{1,9},{2,10},{3,11},{4,12},{5,13},{6,14},{7,15},{8,0},{9,1},... | collective-permute-start | bytes 933896 | tf_op jit(solution)/shard_map/ppermute | solution.py:1044
  16.9 0.0 copy-done.6
  16.9 0.7 collective-permute-start.8
  17.6 0.0 copy-done.3
  17.6 1.8 %shard_map.79 = (f32[3,16,32,128]{3,2,1,0:T(8,128)S(1)}, f32[8,128]{1,0:T(8,128)S(1)}) custom-call(f32[3,16,32,128]{3,2,1,0:T(8,128)S(1)} %bitcast.16, f32[3,3,16,32,128]{4,3,2,1,0:T(8,128)S(1)} %bitcast.11, f32[16,32,128]{2,1,0:T(8,128)S(1)} %bitcast.21, f32[3,16,32,128]{3,2,1,0:T(8,128)S(1)} %bitcast.23, ...), custom_call_target="tpu_custom_call" | custom-call | flops 20000000 | bytes 20000000 | tf_op jit(solution)/shard_map/pallas_call | solution.py:1092
  19.3 0.0 collective-permute-done.4.strain.unit.unit_old
  19.3 0.1 shard_map.81
  19.4 6.9 %collective-permute-start.5 = (f32[9,32,128]{2,1,0:T(8,128)S(1)}, f32[9,32,128]{2,1,0:T(8,128)S(1)}, u32[]{:S(2)}, u32[]{:S(2)}) collective-permute-start(f32[9,32,128]{2,1,0:T(8,128)S(1)} %get-tuple-element.46), channel_id=1, source_target_pairs={{0,8},{1,9},{2,10},{3,11},{4,12},{5,13},{6,14},{7,15},{8,0},{9,1},... | collective-permute-start | bytes 442376 | tf_op jit(solution)/shard_map/ppermute | solution.py:1044
  26.4 0.7 collective-permute-start.6
  27.0 0.0 collective-permute-done.7.fa
  27.0 0.0 collective-permute-done.8.fb
  27.1 2.8 %collective-permute-done.5.xa.refs_0_ = f32[9,32,128]{2,1,0:T(8,128)S(1)} collective-permute-done((f32[9,32,128]{2,1,0:T(8,128)S(1)}, f32[9,32,128]{2,1,0:T(8,128)S(1)}, u32[]{:S(2)}, u32[]{:S(2)}) %collective-permute-start.5) | collective-permute-done | bytes 147488 | tf_op jit(solution)/shard_map/ppermute | solution.py:1044
  29.8 0.0 collective-permute-done.6.xb.refs_1_
  29.8 0.3 shard_map.82
  30.1 2.7 %collective-permute-start.9 = (f32[280,128]{1,0:T(8,128)S(1)}, f32[280,128]{1,0:T(8,128)S(1)}, u32[]{:S(2)}, u32[]{:S(2)}) collective-permute-start(f32[280,128]{1,0:T(8,128)S(1)} %get-tuple-element.50), channel_id=1, source_target_pairs={{0,1},{1,0},{2,3},{3,2},{4,5},{5,4},{6,7},{7,6},{8,9},{9,8},{10,11... | collective-permute-start | bytes 430088 | tf_op jit(solution)/shard_map/ppermute | solution.py:1044
  32.8 0.7 collective-permute-start.10
  33.4 1.2 %shard_map.83 = (f32[12,22,40,128]{3,2,1,0:T(8,128)S(1)}, f32[6,8,40,128]{3,2,1,0:T(8,128)S(1)}) custom-call(f32[3,3,16,32,128]{4,3,2,1,0:T(8,128)S(1)} %bitcast.12, f32[16,32,128]{2,1,0:T(8,128)S(1)} %bitcast.22, f32[3,16,32,128]{3,2,1,0:T(8,128)S(1)} %get-tuple-element.52.tz, s32[1,384]{1,0:T(1,128)S(1)} %reshape.9.layer_map, ...), custom_call_target="tpu_custom_call" | custom-call | flops 30000000 | bytes 30000000 | tf_op jit(solution)/shard_map/pallas_call | solution.py:1098
  34.6 0.7 collective-permute-done.9.refs_2_
  35.3 0.0 collective-permute-done.10.refs_3_
  35.3 2.4 %shard_map.84 = (f32[12,6,40,128]{3,2,1,0:T(8,128)S(1)}, f32[3,22,40,128]{3,2,1,0:T(8,128)S(1)}, f32[3,22,40,128]{3,2,1,0:T(8,128)S(1)}, f32[2,20,40,128]{3,2,1,0:T(8,128)S(1)}) custom-call(f32[3,16,32,128]{3,2,1,0:T(8,128)S(1)} %get-tuple-element.44.residual, f32[16,32,128]{2,1,0:T(8,128)S(1)} %collective-permute-done.4.strain.unit.unit_old, ...), custom_call_target="tpu_custom_call" | custom-call | tf_op jit(solution)/shard_map/pallas_call | solution.py:1109
  37.7 2.5 %collective-permute-start.11 = (f32[2,20,40,128]{3,2,1,0:T(8,128)S(1)}, f32[2,20,40,128]{3,2,1,0:T(8,128)S(1)}, u32[]{:S(2)}, u32[]{:S(2)}) collective-permute-start(f32[2,20,40,128]{3,2,1,0:T(8,128)S(1)} %get-tuple-element.58), channel_id=1, source_target_pairs={{0,64},{1,65},{2,66},{3,67},{4,68},{5,69},{6,70},{7,71},{8,72},{9,... | collective-permute-start | bytes 2457608 | tf_op jit(solution)/shard_map/ppermute | solution.py:1051
  40.2 1.1 %shard_map.85.sums_in = f32[8,128]{1,0:T(8,128)S(1)} custom-call(f32[3,22,40,128]{3,2,1,0:T(8,128)S(1)} %get-tuple-element.55.field.refs_2_, f32[3,22,40,128]{3,2,1,0:T(8,128)S(1)} %get-tuple-element.56.product.refs_3_, f32[12,22,40,128]{3,2,1,0:T(8,128)S(1)} %get-tuple-element.53.refs_4_.faces, f32[3,16,32,128]{3,2,1,0:T(8,128)S(1)} %bitcast.17), custom_call_target="tpu_custom_call" | custom-call | flops 20000000 | bytes 20000000 | tf_op jit(solution)/shard_map/pallas_call | solution.py:1115
  41.3 0.8 %collective-permute-done.11.unit = f32[2,20,40,128]{3,2,1,0:T(8,128)S(1)} collective-permute-done((f32[2,20,40,128]{3,2,1,0:T(8,128)S(1)}, f32[2,20,40,128]{3,2,1,0:T(8,128)S(1)}, u32[]{:S(2)}, u32[]{:S(2)}) %collective-permute-start.11) | collective-permute-done | bytes 819232 | tf_op jit(solution)/shard_map/ppermute | solution.py:1051
  42.2 7.4 %shard_map.86 = (f32[128,128]{1,0:T(8,128)S(1)}, f32[2,3,22,40,128]{4,3,2,1,0:T(8,128)S(1)}, f32[2,3,22,40,128]{4,3,2,1,0:T(8,128)S(1)}) custom-call(f32[3,22,40,128]{3,2,1,0:T(8,128)S(1)} %get-tuple-element.55.field.refs_2_, f32[3,22,40,128]{3,2,1,0:T(8,128)S(1)} %get-tuple-element.56.product.refs_3_, ...), custom_call_target="tpu_custom_call" | custom-call | tf_op jit(solution)/shard_map/pallas_call | solution.py:1118
  49.6 29.2 %all_to_all.11 = f32[128,1,128]{2,1,0:T(1,128)S(1)} all-to-all(f32[128,1,128]{2,1,0:T(1,128)S(1)} %bitcast.25), channel_id=1, replica_groups=mesh['group'=2,'gx'=8,'gy'=8] {'group','gx','gy'}, dimensions={0} | all-to-all | bytes 131072 | tf_op jit(solution)/shard_map/all_to_all | solution.py:1123
  78.7 1.9 %shard_map.87 = (f32[3,16,32,128]{3,2,1,0:T(8,128)}, f32[2]{0:T(128)}) custom-call(f32[128,128]{1,0:T(8,128)S(1)} %bitcast.24, f32[3,16,32,128]{3,2,1,0:T(8,128)S(1)} %bitcast.18, f32[3,22,40,128]{3,2,1,0:T(8,128)S(1)} %get-tuple-element.55.field.refs_2_, f32[3,22,40,128]{3,2,1,0:T(8,128)S(1)} %get-tuple-element.56.product.refs_3_, ...), custom_call_target="tpu_custom_call" | custom-call | tf_op jit(solution)/shard_map/pallas_call | solution.py:1128
  (1 shorter events, 0.0 us)
Async XLA Ops:
  0.6 8.3 %copy-start.4 = (s32[16,32]{1,0:T(8,128)S(1)}, s32[16,32]{1,0:T(8,128)}, u32[]{:S(2)}) copy-start(s32[16,32]{1,0:T(8,128)} %flags_in.1) | copy-start | bytes 6148
  0.6 8.3 %copy-start.2 = (f32[1,16,32,128]{3,2,1,0:T(8,128)S(1)}, f32[1,16,32,128]{3,2,1,0:T(8,128)}, u32[]{:S(2)}) copy-start(f32[1,16,32,128]{3,2,1,0:T(8,128)} %param.8) | copy-start | bytes 786436
  0.7 8.3 %copy-start = (f32[1,3,3,16,32,128]{5,4,3,2,1,0:T(8,128)S(1)}, f32[1,3,3,16,32,128]{5,4,3,2,1,0:T(8,128)}, u32[]{:S(2)}) copy-start(f32[1,3,3,16,32,128]{5,4,3,2,1,0:T(8,128)} %param.7) | copy-start | bytes 7077892
  0.7 8.3 %copy-start.1 = (f32[1,3,16,32,128]{4,3,2,1,0:T(8,128)S(1)}, f32[1,3,16,32,128]{4,3,2,1,0:T(8,128)}, u32[]{:S(2)}) copy-start(f32[1,3,16,32,128]{4,3,2,1,0:T(8,128)} %param.6) | copy-start | bytes 2359300
  0.7 8.2 %copy-start.5 = (s32[384]{0:T(512)S(1)}, s32[384]{0:T(512)}, u32[]{:S(2)}) copy-start(s32[384]{0:T(512)} %param.11) | copy-start | bytes 4612
  4.0 9.1 %copy-start.7 = (f32[19,32,128]{2,1,0:T(8,128)S(1)}, f32[19,32,128]{2,1,0:T(8,128)}, u32[]{:S(2)}) copy-start(f32[19,32,128]{2,1,0:T(8,128)} %get-tuple-element.48) | copy-start | bytes 933892
  4.0 12.8 %copy-start.6 = (f32[19,32,128]{2,1,0:T(8,128)S(1)}, f32[19,32,128]{2,1,0:T(8,128)}, u32[]{:S(2)}) copy-start(f32[19,32,128]{2,1,0:T(8,128)} %get-tuple-element.49) | copy-start | bytes 933892
  4.0 13.5 %copy-start.3 = (f32[1,3,16,32,128]{4,3,2,1,0:T(8,128)S(1)}, f32[1,3,16,32,128]{4,3,2,1,0:T(8,128)}, u32[]{:S(2)}) copy-start(f32[1,3,16,32,128]{4,3,2,1,0:T(8,128)} %param.9) | copy-start | bytes 2359300
  4.1 7.1 %collective-permute-start.2 = (f32[26,16,128]{2,1,0:T(8,128)}, f32[26,16,128]{2,1,0:T(8,128)S(1)}, u32[]{:S(2)}, u32[]{:S(2)}) collective-permute-start(f32[26,16,128]{2,1,0:T(8,128)} %get-tuple-element.36), channel_id=1, source_target_pairs={{0,1},{1,0},{2,3},{3,2},{4,5},{5,4},{6,7},{7,6},{8,9},{9,8},{10,11... | collective-permute-start | bytes 638984 | tf_op jit(solution)/shard_map/ppermute | solution.py:1044
  6.3 4.9 %collective-permute-start.3 = (f32[26,16,128]{2,1,0:T(8,128)}, f32[26,16,128]{2,1,0:T(8,128)S(1)}, u32[]{:S(2)}, u32[]{:S(2)}) collective-permute-start(f32[26,16,128]{2,1,0:T(8,128)} %get-tuple-element.37), channel_id=1, source_target_pairs={{1,2},{2,1},{3,4},{4,3},{5,6},{6,5},{9,10},{10,9},{11,12},{12,11},... | collective-permute-start | bytes 638984 | tf_op jit(solution)/shard_map/ppermute | solution.py:1044
  6.9 4.2 %collective-permute-start = (f32[7,32,128]{2,1,0:T(8,128)}, f32[7,32,128]{2,1,0:T(8,128)S(1)}, u32[]{:S(2)}, u32[]{:S(2)}) collective-permute-start(f32[7,32,128]{2,1,0:T(8,128)} %get-tuple-element.34), channel_id=1, source_target_pairs={{0,8},{1,9},{2,10},{3,11},{4,12},{5,13},{6,14},{7,15},{8,0},{9,1},... | collective-permute-start | bytes 344072 | tf_op jit(solution)/shard_map/ppermute | solution.py:1044
  8.2 2.9 %collective-permute-start.1 = (f32[7,32,128]{2,1,0:T(8,128)}, f32[7,32,128]{2,1,0:T(8,128)S(1)}, u32[]{:S(2)}, u32[]{:S(2)}) collective-permute-start(f32[7,32,128]{2,1,0:T(8,128)} %get-tuple-element.35), channel_id=1, source_target_pairs={{8,16},{9,17},{10,18},{11,19},{12,20},{13,21},{14,22},{15,23},{16,... | collective-permute-start | bytes 344072 | tf_op jit(solution)/shard_map/ppermute | solution.py:1044
  11.3 8.0 %collective-permute-start.4 = (f32[16,32,128]{2,1,0:T(8,128)S(1)}, f32[16,32,128]{2,1,0:T(8,128)S(1)}, u32[]{:S(2)}, u32[]{:S(2)}) collective-permute-start(f32[16,32,128]{2,1,0:T(8,128)S(1)} %shard_map.80), channel_id=1, source_target_pairs={{0,64},{1,65},{2,66},{3,67},{4,68},{5,69},{6,70},{7,71},{8,72},{9,... | collective-permute-start | bytes 786440 | tf_op jit(solution)/shard_map/ppermute | solution.py:1051
  13.1 13.9 %collective-permute-start.7 = (f32[19,32,128]{2,1,0:T(8,128)S(1)}, f32[19,32,128]{2,1,0:T(8,128)S(1)}, u32[]{:S(2)}, u32[]{:S(2)}) collective-permute-start(f32[19,32,128]{2,1,0:T(8,128)S(1)} %copy-done.7), channel_id=1, source_target_pairs={{0,8},{1,9},{2,10},{3,11},{4,12},{5,13},{6,14},{7,15},{8,0},{9,1},... | collective-permute-start | bytes 933896 | tf_op jit(solution)/shard_map/ppermute | solution.py:1044
  16.9 10.2 %collective-permute-start.8 = (f32[19,32,128]{2,1,0:T(8,128)S(1)}, f32[19,32,128]{2,1,0:T(8,128)S(1)}, u32[]{:S(2)}, u32[]{:S(2)}) collective-permute-start(f32[19,32,128]{2,1,0:T(8,128)S(1)} %copy-done.6), channel_id=1, source_target_pairs={{8,16},{9,17},{10,18},{11,19},{12,20},{13,21},{14,22},{15,23},{16,... | collective-permute-start | bytes 933896 | tf_op jit(solution)/shard_map/ppermute | solution.py:1044
  19.4 10.4 %collective-permute-start.5 = (f32[9,32,128]{2,1,0:T(8,128)S(1)}, f32[9,32,128]{2,1,0:T(8,128)S(1)}, u32[]{:S(2)}, u32[]{:S(2)}) collective-permute-start(f32[9,32,128]{2,1,0:T(8,128)S(1)} %get-tuple-element.46), channel_id=1, source_target_pairs={{0,8},{1,9},{2,10},{3,11},{4,12},{5,13},{6,14},{7,15},{8,0},{9,1},... | collective-permute-start | bytes 442376 | tf_op jit(solution)/shard_map/ppermute | solution.py:1044
  26.4 3.4 %collective-permute-start.6 = (f32[9,32,128]{2,1,0:T(8,128)S(1)}, f32[9,32,128]{2,1,0:T(8,128)S(1)}, u32[]{:S(2)}, u32[]{:S(2)}) collective-permute-start(f32[9,32,128]{2,1,0:T(8,128)S(1)} %get-tuple-element.47), channel_id=1, source_target_pairs={{8,16},{9,17},{10,18},{11,19},{12,20},{13,21},{14,22},{15,23},{16,... | collective-permute-start | bytes 442376 | tf_op jit(solution)/shard_map/ppermute | solution.py:1044
  30.1 5.2 %collective-permute-start.9 = (f32[280,128]{1,0:T(8,128)S(1)}, f32[280,128]{1,0:T(8,128)S(1)}, u32[]{:S(2)}, u32[]{:S(2)}) collective-permute-start(f32[280,128]{1,0:T(8,128)S(1)} %get-tuple-element.50), channel_id=1, source_target_pairs={{0,1},{1,0},{2,3},{3,2},{4,5},{5,4},{6,7},{7,6},{8,9},{9,8},{10,11... | collective-permute-start | bytes 430088 | tf_op jit(solution)/shard_map/ppermute | solution.py:1044
  32.8 2.5 %collective-permute-start.10 = (f32[280,128]{1,0:T(8,128)S(1)}, f32[280,128]{1,0:T(8,128)S(1)}, u32[]{:S(2)}, u32[]{:S(2)}) collective-permute-start(f32[280,128]{1,0:T(8,128)S(1)} %get-tuple-element.51), channel_id=1, source_target_pairs={{1,2},{2,1},{3,4},{4,3},{5,6},{6,5},{9,10},{10,9},{11,12},{12,11},... | collective-permute-start | bytes 430088 | tf_op jit(solution)/shard_map/ppermute | solution.py:1044
  37.7 4.5 %collective-permute-start.11 = (f32[2,20,40,128]{3,2,1,0:T(8,128)S(1)}, f32[2,20,40,128]{3,2,1,0:T(8,128)S(1)}, u32[]{:S(2)}, u32[]{:S(2)}) collective-permute-start(f32[2,20,40,128]{3,2,1,0:T(8,128)S(1)} %get-tuple-element.58), channel_id=1, source_target_pairs={{0,64},{1,65},{2,66},{3,67},{4,68},{5,69},{6,70},{7,71},{8,72},{9,... | collective-permute-start | bytes 2457608 | tf_op jit(solution)/shard_map/ppermute | solution.py:1051

commit v2 on v1

--- a/solution.py
+++ b/solution.py
@@ -245,7 +245,7 @@
     loop(0, X, row)
 
 
-def pack_kernel(flags_in, state_in, conduct_in, capacity_in, xa, xb, fa, fb, ya, yb, *scratch):
+def pack_kernel(flags_in, state_in, conduct_in, capacity_in, xa, xb, fb, ya, yb, *scratch):
     flags, state, conduct, capacity, bottom, tz, sem = scratch
     early = [(flags_in, flags)] + [(conduct_in.at[2, k], conduct.at[2, k]) for k in range(3)]
     late = [(conduct_in.at[d, k], conduct.at[d, k]) for d in range(2) for k in range(3)]
@@ -268,7 +268,7 @@
             return tz.at[f - 6]
         return capacity if f == 9 else state.at[f - 10]
 
-    pack_x(source, X_ROWS, Joined(xa, fa), Joined(xb, fb))
+    pack_x(source, X_ROWS, xa, Joined(xb, fb))
     odd = parity("gy")
     for n, (f, r) in enumerate(Y_ROWS):
         put(ya, yb, n, odd, source(f)[:, Y - r, :], source(f)[:, r - 1, :])
@@ -472,9 +472,9 @@
         loop(OX, OX + X, row, (before, x_flux(faces, field, OX - 1)))
 
 
-def halo_kernel(conduct, capacity, tz, layer_map, xa, xb, ya, yb, fa, fb, *refs):
+def halo_kernel(conduct, capacity, tz, layer_map, xa, xb, ya, yb, fb, *refs):
     faces, rim, keep, caps = refs
-    xl, xu, yl, yu = surroundings(Joined(xa, fa), Joined(xb, fb), ya, yb)
+    xl, xu, yl, yu = surroundings(xa, Joined(xb, fb), ya, yb)
     flow = lax.axis_index("group") == 0
 
     def target(f):
@@ -544,10 +544,10 @@
             put(xa, xb, n, odd, unit[X - 1 - depth], unit[depth])
 
 
-def relay_kernel(residual, unit, xa, xb, ka, kb, fa, fb, ya, yb):
+def relay_kernel(residual, unit, xa, xb, ka, kb, fb, ya, yb):
     flow = lax.axis_index("group") == 0
     odd = parity("gy")
-    r_halos, k_halos = lower_upper("gx", xa, xb), lower_upper("gx", Joined(ka, fa), Joined(kb, fb))
+    r_halos, k_halos = lower_upper("gx", xa, xb), lower_upper("gx", ka, Joined(kb, fb))
 
     def give(at, count, ref, index, j):
         put(ya, yb, slice(at, at + count), odd, ref[index(Y - j)], ref[index(j - 1)])
@@ -739,26 +739,27 @@
 
         strains = [strain_row(p, i) for p in products]
         modulus = only(faces[9, i])
-        pushes = [modulus * e for e in strains]
+        later = sorted({b for _, b in pairs})
+        pushes = {b: modulus * strains[b] for b in later}
         for n, (a, b) in enumerate(pairs):
-            add(4 * n + 3, pushes[a] * strains[b])
+            add(4 * n + 3, pushes[b] * strains[a])
         for c in range(3):
             ws = [p[c, i] for p in products]
             dx = [ws[a] - products[a][c, i + 1] for a in vectors]
             dy = [w - up_y(w) for w in ws]
             dz = [w - jnp.where(last, 0.0, up_z(w)) for w in ws]
             sx, sy, sz = (only(faces[3 * d + c, i]) for d in range(3))
-            fx = [sx * d for d in dx]
-            fy = [sy * d for d in dy]
-            fz = [sz * d for d in dz]
+            fx = {b: sx * dx[b] for b in later}
+            fy = {b: sy * dy[b] for b in later}
+            fz = {b: sz * dz[b] for b in later}
+            rs = [f[c, i] for f in fields]
+            r_in = {b: only(rs[b]) for b in later}
+            w_in = {b: only(ws[b]) for b in later}
             for n, (a, b) in enumerate(pairs):
-                add(4 * n + 3, fx[a] * dx[b] + fy[a] * dy[b] + fz[a] * dz[b])
-            rs = [only(f[c, i]) for f in fields]
-            ws = [only(w) for w in ws]
-            for n, (a, b) in enumerate(pairs):
-                add(4 * n, rs[a] * rs[b])
-                add(4 * n + 1, rs[a] * ws[b])
-                add(4 * n + 2, ws[a] * ws[b])
+                add(4 * n + 3, fx[b] * dx[a] + fy[b] * dy[a] + fz[b] * dz[a])
+                add(4 * n, r_in[b] * rs[a])
+                add(4 * n + 1, r_in[b] * ws[a])
+                add(4 * n + 2, w_in[b] * ws[a])
         return carry
 
     loop(OX, OX + X, row, 0, 2)
@@ -1028,21 +1029,22 @@
         loop(0, X, row)
 
 
+def swap(value, start, axis):
+    groups, rows, columns = (lax.axis_size(a) for a in AXES)
+    pairs = []
+    for g in range(groups):
+        for i in range(rows):
+            for j in range(columns):
+                place = i if axis == "gx" else j
+                step = 1 if place % 2 == start else -1
+                if 0 <= place + step < lax.axis_size(axis):
+                    here = (g * rows + i) * columns + j
+                    pairs.append((here, here + step * (columns if axis == "gx" else 1)))
+    return lax.ppermute(value, AXES, pairs)
+
+
 def swaps(first, second, axis):
-    groups, rows, columns = (lax.axis_size(a) for a in AXES)
-    count, found = lax.axis_size(axis), []
-    for value, start in ((first, 0), (second, 1)):
-        pairs = []
-        for g in range(groups):
-            for i in range(rows):
-                for j in range(columns):
-                    place = i if axis == "gx" else j
-                    step = 1 if place % 2 == start else -1
-                    if 0 <= place + step < count:
-                        here = (g * rows + i) * columns + j
-                        pairs.append((here, here + step * (columns if axis == "gx" else 1)))
-        found.append(lax.ppermute(value, AXES, pairs))
-    return found
+    return [swap(first, 0, axis), swap(second, 1, axis)]
 
 
 def core_swap(value):
@@ -1062,9 +1064,10 @@
     full = struct(3, *wide)
 
     y_face = struct(len(Y_ROWS), X, Z)
-    xa, xb, fa, fb, ya, yb = call(
+    x_parts = [struct(n, Y, Z) for n in (len(X_ROWS), len(NEAR), len(X_ROWS) - len(NEAR))]
+    xa, xb, fb, ya, yb = call(
         pack_kernel,
-        x_faces(NEAR) + x_faces(X_ROWS[len(NEAR) :]) + [y_face] * 2,
+        x_parts + [y_face] * 2,
         [
             pltpu.VMEM((X, Y), jnp.int32),
             pltpu.VMEM((3, X, Y, Z), F32),
@@ -1079,7 +1082,7 @@
         count=4,
     )(flags, state, conduct, capacity)
     k_halos = lax.optimization_barrier(swaps(xa, xb, "gx") + swaps(ya, yb, "gy"))
-    far = swaps(fa, fb, "gx")
+    far = swap(fb, 1, "gx")
     wide_faces = struct(12, *wide)
     tables = [pltpu.VMEM((6, *wide), F32), pltpu.VMEM(wide, F32)]
     inner, tz, unit0 = call(
@@ -1097,13 +1100,13 @@
     )(state, conduct, capacity, supply, inner, *k_halos)
     faces, k_rim = call(
         halo_kernel, [wide_faces, struct(6, len(K_RIM), EY, Z)], tables, cost=30_000_000
-    )(conduct, capacity, tz, layer_map, *k_halos, *far)
+    )(conduct, capacity, tz, layer_map, *k_halos, far)
     residual, xa, xb = call(residual_kernel, [tile] + x_faces(R_ROWS))(
         base, cross, cross, layer_map
     )
     halos = swaps(xa, xb, "gx")
     ya, yb = call(relay_kernel, [struct(Y_PACK, Z)] * 2)(
-        residual, cross, *halos, k_halos[0], k_halos[1], *far
+        residual, cross, *halos, k_halos[0], k_halos[1], far
     )
     halos = halos + swaps(ya, yb, "gy")
     rim, field, product, unit12 = call(

time: 80.9 us -> 80.9 us (level)
  starting transfers between devices: 24.5 us -> 16.8 us
  waiting for transfers between devices: 5.04 us -> 10.4 us
  blocking collectives: 29.2 us -> 31.6 us
    ppermute x10 -> x9, starting transfers between devices: 20.2 us -> 13.2 us  [swap(): return lax.ppermute(value, AXES, pairs)]
    ppermute x10 -> x9, waiting for transfers between devices: 4.2 us -> 9.53 us  [swap(): return lax.ppermute(value, AXES, pairs)]
    all_to_all x1, blocking collectives: 29.2 us -> 31.6 us  [body(): sums = lax.all_to_all(sums, AXES, 0, 0, tiled=True)]
  transfers between devices with their start and end apart: 12 -> 11, of which waited for: 4 -> 5; matrix products, arithmetic and copies ran while one was open for 0% -> 0% of each run, Pallas kernels for 7% -> 7%
where the time goes in v2:
time: 80.9 us; the launch traced here: 80.7 us
  blocking collectives  31.6 us (39%)
  Pallas kernels  21 us (26%)
  starting transfers between devices  16.8 us (21%)
  waiting for transfers between devices  10.4 us (13%)
  between operations  0.89 us (1%)
    all_to_all x1, blocking collectives, body(): sums = lax.all_to_all(sums, AXES, 0, 0, tiled=True)  31.6 us
    ppermute x9, starting transfers between devices, swap(): return lax.ppermute(value, AXES, pairs)  13.2 us
    ppermute x9, waiting for transfers between devices, swap(): return lax.ppermute(value, AXES, pairs)  9.53 us
    pallas_call x1, Pallas kernels, body(): call(sums_kernel, [struct(devices, Z), struct(2, 3, *wide), struct(2, 3,...  7.23 us
    ppermute x2, starting transfers between devices, core_swap(): return lax.ppermute(value, AXES, pairs)  3.58 us
    pallas_call x1, Pallas kernels, body(): call(pack_kernel, x_parts + [y_face] * 2, [pltpu.VMEM((X, Y), jnp.int32),...  3.47 us
    pallas_call x1, Pallas kernels, body(): call(image_kernel, [struct(12, len(RIM), EY, Z), full, full, struct(2, EX...  2.42 us
    pallas_call x1, Pallas kernels, body(): call(finish, [tile, struct(2)], scalars=(1,))  1.93 us
  transfers between devices with their start and end apart: 11, of which 5 were waited for; matrix products, arithmetic and copies ran while one was open for 0% of the time, Pallas kernels for 7%

profile of v2, /device:TPU:1, one launch (start us, length us, event | category | flops | bytes accessed | tf_op | source)
XLA Modules:
  0.0 80.7 jit_solution(10892318413084231132)
XLA Ops:
  0.6 0.0 copy-start.4
  0.6 0.0 copy-start.2
  0.7 0.0 copy-start
  0.7 0.0 copy-start.1
  0.7 0.0 copy-start.5
  0.7 3.5 %shard_map.78 = (f32[26,32,128]{2,1,0:T(8,128)}, f32[7,32,128]{2,1,0:T(8,128)}, f32[19,32,128]{2,1,0:T(8,128)}, f32[26,16,128]{2,1,0:T(8,128)}, f32[26,16,128]{2,1,0:T(8,128)}) custom-call(s32[16,32]{1,0:T(8,128)} %flags_in.1, f32[3,16,32,128]{3,2,1,0:T(8,128)} %bitcast.13, f32[3,3,16,32,128]{4,3,2,1,0:T(8,128)} %bitcast.9, f32[16,32,128]{2,1,0:T(8,128)} %bitcast.19), custom_call_target="tpu_custom_call" | custom-call | tf_op jit(solution)/shard_map/pallas_call | solution.py:1068
  4.2 2.1 %collective-permute-start = (f32[26,32,128]{2,1,0:T(8,128)}, f32[26,32,128]{2,1,0:T(8,128)S(1)}, u32[]{:S(2)}, u32[]{:S(2)}) collective-permute-start(f32[26,32,128]{2,1,0:T(8,128)} %get-tuple-element.33), channel_id=1, source_target_pairs={{0,8},{1,9},{2,10},{3,11},{4,12},{5,13},{6,14},{7,15},{8,0},{9,1},... | collective-permute-start | bytes 1277960 | tf_op jit(solution)/shard_map/ppermute | solution.py:1043
  6.3 1.3 %collective-permute-start.2 = (f32[26,16,128]{2,1,0:T(8,128)}, f32[26,16,128]{2,1,0:T(8,128)S(1)}, u32[]{:S(2)}, u32[]{:S(2)}) collective-permute-start(f32[26,16,128]{2,1,0:T(8,128)} %get-tuple-element.35), channel_id=1, source_target_pairs={{0,1},{1,0},{2,3},{3,2},{4,5},{5,4},{6,7},{7,6},{8,9},{9,8},{10,11... | collective-permute-start | bytes 638984 | tf_op jit(solution)/shard_map/ppermute | solution.py:1043
  7.6 0.7 collective-permute-start.3
  8.2 0.7 collective-permute-start.1
  8.9 0.0 copy-done.5
  8.9 0.0 copy-done.4
  9.0 0.0 copy-done.2
  9.0 0.0 copy-done
  9.0 0.0 copy-done.1
  9.0 0.0 copy-start.6
  9.0 0.0 copy-start.3
  9.0 1.4 %shard_map.77 = (f32[12,22,40,128]{3,2,1,0:T(8,128)S(1)}, f32[3,16,32,128]{3,2,1,0:T(8,128)S(1)}, f32[16,32,128]{2,1,0:T(8,128)S(1)}) custom-call(f32[3,16,32,128]{3,2,1,0:T(8,128)S(1)} %bitcast.14, f32[3,3,16,32,128]{4,3,2,1,0:T(8,128)S(1)} %bitcast.10, f32[16,32,128]{2,1,0:T(8,128)S(1)} %bitcast.20, s32[16,32]{1,0:T(8,128)S(1)} %copy-done.4, ...), custom_call_target="tpu_custom_call" | custom-call | flops 30000000 | bytes 30000000 | tf_op jit(solution)/shard_map/pallas_call | solution.py:1088
  10.4 0.0 collective-permute-done.1.xb.kb
  10.5 1.8 %collective-permute-done.2.ya = f32[26,16,128]{2,1,0:T(8,128)S(1)} collective-permute-done((f32[26,16,128]{2,1,0:T(8,128)}, f32[26,16,128]{2,1,0:T(8,128)S(1)}, u32[]{:S(2)}, u32[]{:S(2)}) %collective-permute-start.2) | collective-permute-done | bytes 213024 | tf_op jit(solution)/shard_map/ppermute | solution.py:1043
  12.3 0.0 collective-permute-done.3.yb
  12.3 3.2 %collective-permute-done.xa.ka = f32[26,32,128]{2,1,0:T(8,128)S(1)} collective-permute-done((f32[26,32,128]{2,1,0:T(8,128)}, f32[26,32,128]{2,1,0:T(8,128)S(1)}, u32[]{:S(2)}, u32[]{:S(2)}) %collective-permute-start) | collective-permute-done | bytes 426016 | tf_op jit(solution)/shard_map/ppermute | solution.py:1043
  15.5 0.1 shard_map.80
  15.7 1.7 %collective-permute-start.4 = (f32[16,32,128]{2,1,0:T(8,128)S(1)}, f32[16,32,128]{2,1,0:T(8,128)S(1)}, u32[]{:S(2)}, u32[]{:S(2)}) collective-permute-start(f32[16,32,128]{2,1,0:T(8,128)S(1)} %shard_map.80), channel_id=1, source_target_pairs={{0,64},{1,65},{2,66},{3,67},{4,68},{5,69},{6,70},{7,71},{8,72},{9,... | collective-permute-start | bytes 786440 | tf_op jit(solution)/shard_map/ppermute | solution.py:1053
  17.4 0.0 copy-done.6
  17.4 0.7 collective-permute-start.7
  18.1 0.0 copy-done.3
  18.1 1.7 %shard_map.79 = (f32[3,16,32,128]{3,2,1,0:T(8,128)S(1)}, f32[8,128]{1,0:T(8,128)S(1)}) custom-call(f32[3,16,32,128]{3,2,1,0:T(8,128)S(1)} %bitcast.16, f32[3,3,16,32,128]{4,3,2,1,0:T(8,128)S(1)} %bitcast.11, f32[16,32,128]{2,1,0:T(8,128)S(1)} %bitcast.21, f32[3,16,32,128]{3,2,1,0:T(8,128)S(1)} %bitcast.23, ...), custom_call_target="tpu_custom_call" | custom-call | flops 20000000 | bytes 20000000 | tf_op jit(solution)/shard_map/pallas_call | solution.py:1095
  19.8 0.0 collective-permute-done.4.strain.unit.unit_old
  19.8 0.1 shard_map.81
  19.9 4.0 %collective-permute-start.5 = (f32[9,32,128]{2,1,0:T(8,128)S(1)}, f32[9,32,128]{2,1,0:T(8,128)S(1)}, u32[]{:S(2)}, u32[]{:S(2)}) collective-permute-start(f32[9,32,128]{2,1,0:T(8,128)S(1)} %get-tuple-element.45), channel_id=1, source_target_pairs={{0,8},{1,9},{2,10},{3,11},{4,12},{5,13},{6,14},{7,15},{8,0},{9,1},... | collective-permute-start | bytes 442376 | tf_op jit(solution)/shard_map/ppermute | solution.py:1043
  23.9 0.7 collective-permute-start.6
  24.6 0.0 collective-permute-done.7.fb
  24.6 3.1 %collective-permute-done.5.xa.refs_0_ = f32[9,32,128]{2,1,0:T(8,128)S(1)} collective-permute-done((f32[9,32,128]{2,1,0:T(8,128)S(1)}, f32[9,32,128]{2,1,0:T(8,128)S(1)}, u32[]{:S(2)}, u32[]{:S(2)}) %collective-permute-start.5) | collective-permute-done | bytes 147488 | tf_op jit(solution)/shard_map/ppermute | solution.py:1043
  27.7 0.0 collective-permute-done.6.xb.refs_1_
  27.7 0.3 shard_map.82
  28.0 2.5 %collective-permute-start.8 = (f32[280,128]{1,0:T(8,128)S(1)}, f32[280,128]{1,0:T(8,128)S(1)}, u32[]{:S(2)}, u32[]{:S(2)}) collective-permute-start(f32[280,128]{1,0:T(8,128)S(1)} %get-tuple-element.48), channel_id=1, source_target_pairs={{0,1},{1,0},{2,3},{3,2},{4,5},{5,4},{6,7},{7,6},{8,9},{9,8},{10,11... | collective-permute-start | bytes 430088 | tf_op jit(solution)/shard_map/ppermute | solution.py:1043
  30.5 0.7 collective-permute-start.9
  31.2 1.2 %shard_map.83 = (f32[12,22,40,128]{3,2,1,0:T(8,128)S(1)}, f32[6,8,40,128]{3,2,1,0:T(8,128)S(1)}) custom-call(f32[3,3,16,32,128]{4,3,2,1,0:T(8,128)S(1)} %bitcast.12, f32[16,32,128]{2,1,0:T(8,128)S(1)} %bitcast.22, f32[3,16,32,128]{3,2,1,0:T(8,128)S(1)} %get-tuple-element.50.tz, s32[1,384]{1,0:T(1,128)S(1)} %reshape.9.layer_map, ...), custom_call_target="tpu_custom_call" | custom-call | flops 30000000 | bytes 30000000 | tf_op jit(solution)/shard_map/pallas_call | solution.py:1101
  32.3 1.3 %collective-permute-done.8.refs_2_ = f32[280,128]{1,0:T(8,128)S(1)} collective-permute-done((f32[280,128]{1,0:T(8,128)S(1)}, f32[280,128]{1,0:T(8,128)S(1)}, u32[]{:S(2)}, u32[]{:S(2)}) %collective-permute-start.8) | collective-permute-done | bytes 143392 | tf_op jit(solution)/shard_map/ppermute | solution.py:1043
  33.7 0.0 collective-permute-done.9.refs_3_
  33.7 2.4 %shard_map.84 = (f32[12,6,40,128]{3,2,1,0:T(8,128)S(1)}, f32[3,22,40,128]{3,2,1,0:T(8,128)S(1)}, f32[3,22,40,128]{3,2,1,0:T(8,128)S(1)}, f32[2,20,40,128]{3,2,1,0:T(8,128)S(1)}) custom-call(f32[3,16,32,128]{3,2,1,0:T(8,128)S(1)} %get-tuple-element.43.residual, f32[16,32,128]{2,1,0:T(8,128)S(1)} %collective-permute-done.4.strain.unit.unit_old, ...), custom_call_target="tpu_custom_call" | custom-call | tf_op jit(solution)/shard_map/pallas_call | solution.py:1112
  36.1 1.9 %collective-permute-start.10 = (f32[2,20,40,128]{3,2,1,0:T(8,128)S(1)}, f32[2,20,40,128]{3,2,1,0:T(8,128)S(1)}, u32[]{:S(2)}, u32[]{:S(2)}) collective-permute-start(f32[2,20,40,128]{3,2,1,0:T(8,128)S(1)} %get-tuple-element.56), channel_id=1, source_target_pairs={{0,64},{1,65},{2,66},{3,67},{4,68},{5,69},{6,70},{7,71},{8,72},{9,... | collective-permute-start | bytes 2457608 | tf_op jit(solution)/shard_map/ppermute | solution.py:1053
  38.0 1.1 %shard_map.85.sums_in = f32[8,128]{1,0:T(8,128)S(1)} custom-call(f32[3,22,40,128]{3,2,1,0:T(8,128)S(1)} %get-tuple-element.53.field.refs_2_, f32[3,22,40,128]{3,2,1,0:T(8,128)S(1)} %get-tuple-element.54.product.refs_3_, f32[12,22,40,128]{3,2,1,0:T(8,128)S(1)} %get-tuple-element.51.refs_4_.faces, f32[3,16,32,128]{3,2,1,0:T(8,128)S(1)} %bitcast.17), custom_call_target="tpu_custom_call" | custom-call | flops 20000000 | bytes 20000000 | tf_op jit(solution)/shard_map/pallas_call | solution.py:1118
  39.1 0.8 %collective-permute-done.10.unit = f32[2,20,40,128]{3,2,1,0:T(8,128)S(1)} collective-permute-done((f32[2,20,40,128]{3,2,1,0:T(8,128)S(1)}, f32[2,20,40,128]{3,2,1,0:T(8,128)S(1)}, u32[]{:S(2)}, u32[]{:S(2)}) %collective-permute-start.10) | collective-permute-done | bytes 819232 | tf_op jit(solution)/shard_map/ppermute | solution.py:1053
  39.9 7.2 %shard_map.86 = (f32[128,128]{1,0:T(8,128)S(1)}, f32[2,3,22,40,128]{4,3,2,1,0:T(8,128)S(1)}, f32[2,3,22,40,128]{4,3,2,1,0:T(8,128)S(1)}) custom-call(f32[3,22,40,128]{3,2,1,0:T(8,128)S(1)} %get-tuple-element.53.field.refs_2_, f32[3,22,40,128]{3,2,1,0:T(8,128)S(1)} %get-tuple-element.54.product.refs_3_, ...), custom_call_target="tpu_custom_call" | custom-call | tf_op jit(solution)/shard_map/pallas_call | solution.py:1121
  47.2 31.6 %all_to_all.11 = f32[128,1,128]{2,1,0:T(1,128)S(1)} all-to-all(f32[128,1,128]{2,1,0:T(1,128)S(1)} %bitcast.25), channel_id=1, replica_groups=mesh['group'=2,'gx'=8,'gy'=8] {'group','gx','gy'}, dimensions={0} | all-to-all | bytes 131072 | tf_op jit(solution)/shard_map/all_to_all | solution.py:1126
  78.8 1.9 %shard_map.87 = (f32[3,16,32,128]{3,2,1,0:T(8,128)}, f32[2]{0:T(128)}) custom-call(f32[128,128]{1,0:T(8,128)S(1)} %bitcast.24, f32[3,16,32,128]{3,2,1,0:T(8,128)S(1)} %bitcast.18, f32[3,22,40,128]{3,2,1,0:T(8,128)S(1)} %get-tuple-element.53.field.refs_2_, f32[3,22,40,128]{3,2,1,0:T(8,128)S(1)} %get-tuple-element.54.product.refs_3_, ...), custom_call_target="tpu_custom_call" | custom-call | tf_op jit(solution)/shard_map/pallas_call | solution.py:1131
  (1 shorter events, 0.0 us)
Async XLA Ops:
  0.6 8.3 %copy-start.4 = (s32[16,32]{1,0:T(8,128)S(1)}, s32[16,32]{1,0:T(8,128)}, u32[]{:S(2)}) copy-start(s32[16,32]{1,0:T(8,128)} %flags_in.1) | copy-start | bytes 6148
  0.6 8.3 %copy-start.2 = (f32[1,16,32,128]{3,2,1,0:T(8,128)S(1)}, f32[1,16,32,128]{3,2,1,0:T(8,128)}, u32[]{:S(2)}) copy-start(f32[1,16,32,128]{3,2,1,0:T(8,128)} %param.8) | copy-start | bytes 786436
  0.7 8.3 %copy-start = (f32[1,3,3,16,32,128]{5,4,3,2,1,0:T(8,128)S(1)}, f32[1,3,3,16,32,128]{5,4,3,2,1,0:T(8,128)}, u32[]{:S(2)}) copy-start(f32[1,3,3,16,32,128]{5,4,3,2,1,0:T(8,128)} %param.7) | copy-start | bytes 7077892
  0.7 8.3 %copy-start.1 = (f32[1,3,16,32,128]{4,3,2,1,0:T(8,128)S(1)}, f32[1,3,16,32,128]{4,3,2,1,0:T(8,128)}, u32[]{:S(2)}) copy-start(f32[1,3,16,32,128]{4,3,2,1,0:T(8,128)} %param.6) | copy-start | bytes 2359300
  0.7 8.3 %copy-start.5 = (s32[384]{0:T(512)S(1)}, s32[384]{0:T(512)}, u32[]{:S(2)}) copy-start(s32[384]{0:T(512)} %param.11) | copy-start | bytes 4612
  4.2 11.4 %collective-permute-start = (f32[26,32,128]{2,1,0:T(8,128)}, f32[26,32,128]{2,1,0:T(8,128)S(1)}, u32[]{:S(2)}, u32[]{:S(2)}) collective-permute-start(f32[26,32,128]{2,1,0:T(8,128)} %get-tuple-element.33), channel_id=1, source_target_pairs={{0,8},{1,9},{2,10},{3,11},{4,12},{5,13},{6,14},{7,15},{8,0},{9,1},... | collective-permute-start | bytes 1277960 | tf_op jit(solution)/shard_map/ppermute | solution.py:1043
  6.3 6.0 %collective-permute-start.2 = (f32[26,16,128]{2,1,0:T(8,128)}, f32[26,16,128]{2,1,0:T(8,128)S(1)}, u32[]{:S(2)}, u32[]{:S(2)}) collective-permute-start(f32[26,16,128]{2,1,0:T(8,128)} %get-tuple-element.35), channel_id=1, source_target_pairs={{0,1},{1,0},{2,3},{3,2},{4,5},{5,4},{6,7},{7,6},{8,9},{9,8},{10,11... | collective-permute-start | bytes 638984 | tf_op jit(solution)/shard_map/ppermute | solution.py:1043
  7.6 4.7 %collective-permute-start.3 = (f32[26,16,128]{2,1,0:T(8,128)}, f32[26,16,128]{2,1,0:T(8,128)S(1)}, u32[]{:S(2)}, u32[]{:S(2)}) collective-permute-start(f32[26,16,128]{2,1,0:T(8,128)} %get-tuple-element.36), channel_id=1, source_target_pairs={{1,2},{2,1},{3,4},{4,3},{5,6},{6,5},{9,10},{10,9},{11,12},{12,11},... | collective-permute-start | bytes 638984 | tf_op jit(solution)/shard_map/ppermute | solution.py:1043
  8.2 2.2 %collective-permute-start.1 = (f32[7,32,128]{2,1,0:T(8,128)}, f32[7,32,128]{2,1,0:T(8,128)S(1)}, u32[]{:S(2)}, u32[]{:S(2)}) collective-permute-start(f32[7,32,128]{2,1,0:T(8,128)} %get-tuple-element.34), channel_id=1, source_target_pairs={{8,16},{9,17},{10,18},{11,19},{12,20},{13,21},{14,22},{15,23},{16,... | collective-permute-start | bytes 344072 | tf_op jit(solution)/shard_map/ppermute | solution.py:1043
  9.0 8.4 %copy-start.6 = (f32[19,32,128]{2,1,0:T(8,128)S(1)}, f32[19,32,128]{2,1,0:T(8,128)}, u32[]{:S(2)}) copy-start(f32[19,32,128]{2,1,0:T(8,128)} %get-tuple-element.47) | copy-start | bytes 933892
  9.0 9.1 %copy-start.3 = (f32[1,3,16,32,128]{4,3,2,1,0:T(8,128)S(1)}, f32[1,3,16,32,128]{4,3,2,1,0:T(8,128)}, u32[]{:S(2)}) copy-start(f32[1,3,16,32,128]{4,3,2,1,0:T(8,128)} %param.9) | copy-start | bytes 2359300
  15.7 4.2 %collective-permute-start.4 = (f32[16,32,128]{2,1,0:T(8,128)S(1)}, f32[16,32,128]{2,1,0:T(8,128)S(1)}, u32[]{:S(2)}, u32[]{:S(2)}) collective-permute-start(f32[16,32,128]{2,1,0:T(8,128)S(1)} %shard_map.80), channel_id=1, source_target_pairs={{0,64},{1,65},{2,66},{3,67},{4,68},{5,69},{6,70},{7,71},{8,72},{9,... | collective-permute-start | bytes 786440 | tf_op jit(solution)/shard_map/ppermute | solution.py:1053
  17.4 7.2 %collective-permute-start.7 = (f32[19,32,128]{2,1,0:T(8,128)S(1)}, f32[19,32,128]{2,1,0:T(8,128)S(1)}, u32[]{:S(2)}, u32[]{:S(2)}) collective-permute-start(f32[19,32,128]{2,1,0:T(8,128)S(1)} %copy-done.6), channel_id=1, source_target_pairs={{8,16},{9,17},{10,18},{11,19},{12,20},{13,21},{14,22},{15,23},{16,... | collective-permute-start | bytes 933896 | tf_op jit(solution)/shard_map/ppermute | solution.py:1043
  19.9 7.8 %collective-permute-start.5 = (f32[9,32,128]{2,1,0:T(8,128)S(1)}, f32[9,32,128]{2,1,0:T(8,128)S(1)}, u32[]{:S(2)}, u32[]{:S(2)}) collective-permute-start(f32[9,32,128]{2,1,0:T(8,128)S(1)} %get-tuple-element.45), channel_id=1, source_target_pairs={{0,8},{1,9},{2,10},{3,11},{4,12},{5,13},{6,14},{7,15},{8,0},{9,1},... | collective-permute-start | bytes 442376 | tf_op jit(solution)/shard_map/ppermute | solution.py:1043
  23.9 3.8 %collective-permute-start.6 = (f32[9,32,128]{2,1,0:T(8,128)S(1)}, f32[9,32,128]{2,1,0:T(8,128)S(1)}, u32[]{:S(2)}, u32[]{:S(2)}) collective-permute-start(f32[9,32,128]{2,1,0:T(8,128)S(1)} %get-tuple-element.46), channel_id=1, source_target_pairs={{8,16},{9,17},{10,18},{11,19},{12,20},{13,21},{14,22},{15,23},{16,... | collective-permute-start | bytes 442376 | tf_op jit(solution)/shard_map/ppermute | solution.py:1043
  28.0 5.7 %collective-permute-start.8 = (f32[280,128]{1,0:T(8,128)S(1)}, f32[280,128]{1,0:T(8,128)S(1)}, u32[]{:S(2)}, u32[]{:S(2)}) collective-permute-start(f32[280,128]{1,0:T(8,128)S(1)} %get-tuple-element.48), channel_id=1, source_target_pairs={{0,1},{1,0},{2,3},{3,2},{4,5},{5,4},{6,7},{7,6},{8,9},{9,8},{10,11... | collective-permute-start | bytes 430088 | tf_op jit(solution)/shard_map/ppermute | solution.py:1043
  30.5 3.2 %collective-permute-start.9 = (f32[280,128]{1,0:T(8,128)S(1)}, f32[280,128]{1,0:T(8,128)S(1)}, u32[]{:S(2)}, u32[]{:S(2)}) collective-permute-start(f32[280,128]{1,0:T(8,128)S(1)} %get-tuple-element.49), channel_id=1, source_target_pairs={{1,2},{2,1},{3,4},{4,3},{5,6},{6,5},{9,10},{10,9},{11,12},{12,11},... | collective-permute-start | bytes 430088 | tf_op jit(solution)/shard_map/ppermute | solution.py:1043
  36.1 3.8 %collective-permute-start.10 = (f32[2,20,40,128]{3,2,1,0:T(8,128)S(1)}, f32[2,20,40,128]{3,2,1,0:T(8,128)S(1)}, u32[]{:S(2)}, u32[]{:S(2)}) collective-permute-start(f32[2,20,40,128]{3,2,1,0:T(8,128)S(1)} %get-tuple-element.56), channel_id=1, source_target_pairs={{0,64},{1,65},{2,66},{3,67},{4,68},{5,69},{6,70},{7,71},{8,72},{9,... | collective-permute-start | bytes 2457608 | tf_op jit(solution)/shard_map/ppermute | solution.py:1053

commit v3 on v1

--- a/solution.py
+++ b/solution.py
@@ -739,26 +739,27 @@
 
         strains = [strain_row(p, i) for p in products]
         modulus = only(faces[9, i])
-        pushes = [modulus * e for e in strains]
+        later = sorted({b for _, b in pairs})
+        pushes = {b: modulus * strains[b] for b in later}
         for n, (a, b) in enumerate(pairs):
-            add(4 * n + 3, pushes[a] * strains[b])
+            add(4 * n + 3, pushes[b] * strains[a])
         for c in range(3):
             ws = [p[c, i] for p in products]
             dx = [ws[a] - products[a][c, i + 1] for a in vectors]
             dy = [w - up_y(w) for w in ws]
             dz = [w - jnp.where(last, 0.0, up_z(w)) for w in ws]
             sx, sy, sz = (only(faces[3 * d + c, i]) for d in range(3))
-            fx = [sx * d for d in dx]
-            fy = [sy * d for d in dy]
-            fz = [sz * d for d in dz]
+            fx = {b: sx * dx[b] for b in later}
+            fy = {b: sy * dy[b] for b in later}
+            fz = {b: sz * dz[b] for b in later}
+            rs = [f[c, i] for f in fields]
+            r_in = {b: only(rs[b]) for b in later}
+            w_in = {b: only(ws[b]) for b in later}
             for n, (a, b) in enumerate(pairs):
-                add(4 * n + 3, fx[a] * dx[b] + fy[a] * dy[b] + fz[a] * dz[b])
-            rs = [only(f[c, i]) for f in fields]
-            ws = [only(w) for w in ws]
-            for n, (a, b) in enumerate(pairs):
-                add(4 * n, rs[a] * rs[b])
-                add(4 * n + 1, rs[a] * ws[b])
-                add(4 * n + 2, ws[a] * ws[b])
+                add(4 * n + 3, fx[b] * dx[a] + fy[b] * dy[a] + fz[b] * dz[a])
+                add(4 * n, r_in[b] * rs[a])
+                add(4 * n + 1, r_in[b] * ws[a])
+                add(4 * n + 2, w_in[b] * ws[a])
         return carry
 
     loop(OX, OX + X, row, 0, 2)

time: 80.9 us -> 80.8 us (level)
  no operation moved by 1% of the time
where the time goes in v3:
time: 80.8 us; the launch traced here: 80.5 us
  blocking collectives  29.2 us (36%)
  starting transfers between devices  24.5 us (30%)
  Pallas kernels  20.9 us (26%)
  waiting for transfers between devices  5.04 us (6%)
  between operations  0.9 us (1%)
    all_to_all x1, blocking collectives, body(): sums = lax.all_to_all(sums, AXES, 0, 0, tiled=True)  29.2 us
    ppermute x10, starting transfers between devices, swaps(): found.append(lax.ppermute(value, AXES, pairs))  20.2 us
    pallas_call x1, Pallas kernels, body(): call(sums_kernel, [struct(devices, Z), struct(2, 3, *wide), struct(2, 3,...  7.23 us
    ppermute x2, starting transfers between devices, core_swap(): return lax.ppermute(value, AXES, pairs)  4.3 us
    ppermute x10, waiting for transfers between devices, swaps(): found.append(lax.ppermute(value, AXES, pairs))  4.2 us
    pallas_call x1, Pallas kernels, body(): call(pack_kernel, x_faces(NEAR) + x_faces(X_ROWS[len(NEAR):]) + [y_face]...  3.34 us
    pallas_call x1, Pallas kernels, body(): call(image_kernel, [struct(12, len(RIM), EY, Z), full, full, struct(2, EX...  2.42 us
    pallas_call x1, Pallas kernels, body(): call(finish, [tile, struct(2)], scalars=(1,))  1.93 us
  transfers between devices with their start and end apart: 12, of which 4 were waited for; matrix products, arithmetic and copies ran while one was open for 0% of the time, Pallas kernels for 7%

profile of v3, /device:TPU:1, one launch (start us, length us, event | category | flops | bytes accessed | tf_op | source)
XLA Modules:
  0.0 80.5 jit_solution(2073350939097695086)
XLA Ops:
  0.6 0.0 copy-start.4
  0.6 0.0 copy-start.2
  0.7 0.0 copy-start
  0.7 0.0 copy-start.1
  0.7 0.0 copy-start.5
  0.7 3.3 %shard_map.78 = (f32[7,32,128]{2,1,0:T(8,128)}, f32[7,32,128]{2,1,0:T(8,128)}, f32[19,32,128]{2,1,0:T(8,128)}, f32[19,32,128]{2,1,0:T(8,128)}, f32[26,16,128]{2,1,0:T(8,128)}, /*index=5*/f32[26,16,128]{2,1,0:T(8,128)}) custom-call(s32[16,32]{1,0:T(8,128)} %flags_in.1, f32[3,16,32,128]{3,2,1,0:T(8,128)} %bitcast.13, f32[3,3,16,32,128]{4,3,2,1,0:T(8,128)} %bitcast.9, ...), custom_call_target="tpu_custom_call" | custom-call | tf_op jit(solution)/shard_map/pallas_call | solution.py:1066
  4.0 0.0 copy-start.7
  4.0 0.0 copy-start.6
  4.0 0.0 copy-start.3
  4.1 2.2 %collective-permute-start.2 = (f32[26,16,128]{2,1,0:T(8,128)}, f32[26,16,128]{2,1,0:T(8,128)S(1)}, u32[]{:S(2)}, u32[]{:S(2)}) collective-permute-start(f32[26,16,128]{2,1,0:T(8,128)} %get-tuple-element.36), channel_id=1, source_target_pairs={{0,1},{1,0},{2,3},{3,2},{4,5},{5,4},{6,7},{7,6},{8,9},{9,8},{10,11... | collective-permute-start | bytes 638984 | tf_op jit(solution)/shard_map/ppermute | solution.py:1045
  6.3 0.7 collective-permute-start.3
  6.9 1.3 %collective-permute-start = (f32[7,32,128]{2,1,0:T(8,128)}, f32[7,32,128]{2,1,0:T(8,128)S(1)}, u32[]{:S(2)}, u32[]{:S(2)}) collective-permute-start(f32[7,32,128]{2,1,0:T(8,128)} %get-tuple-element.34), channel_id=1, source_target_pairs={{0,8},{1,9},{2,10},{3,11},{4,12},{5,13},{6,14},{7,15},{8,0},{9,1},... | collective-permute-start | bytes 344072 | tf_op jit(solution)/shard_map/ppermute | solution.py:1045
  8.2 0.7 collective-permute-start.1
  8.9 0.0 copy-done.5
  8.9 0.0 copy-done.4
  8.9 0.0 copy-done.2
  8.9 0.0 copy-done
  8.9 0.0 copy-done.1
  9.0 1.4 %shard_map.77 = (f32[12,22,40,128]{3,2,1,0:T(8,128)S(1)}, f32[3,16,32,128]{3,2,1,0:T(8,128)S(1)}, f32[16,32,128]{2,1,0:T(8,128)S(1)}) custom-call(f32[3,16,32,128]{3,2,1,0:T(8,128)S(1)} %bitcast.14, f32[3,3,16,32,128]{4,3,2,1,0:T(8,128)S(1)} %bitcast.10, f32[16,32,128]{2,1,0:T(8,128)S(1)} %bitcast.20, s32[16,32]{1,0:T(8,128)S(1)} %copy-done.4, ...), custom_call_target="tpu_custom_call" | custom-call | flops 30000000 | bytes 30000000 | tf_op jit(solution)/shard_map/pallas_call | solution.py:1086
  10.4 0.8 collective-permute-done.xa.ka
  11.2 0.0 collective-permute-done.1.xb.kb
  11.2 0.0 collective-permute-done.2.ya
  11.2 0.0 collective-permute-done.3.yb
  11.2 0.2 shard_map.80
  11.3 1.8 %collective-permute-start.4 = (f32[16,32,128]{2,1,0:T(8,128)S(1)}, f32[16,32,128]{2,1,0:T(8,128)S(1)}, u32[]{:S(2)}, u32[]{:S(2)}) collective-permute-start(f32[16,32,128]{2,1,0:T(8,128)S(1)} %shard_map.80), channel_id=1, source_target_pairs={{0,64},{1,65},{2,66},{3,67},{4,68},{5,69},{6,70},{7,71},{8,72},{9,... | collective-permute-start | bytes 786440 | tf_op jit(solution)/shard_map/ppermute | solution.py:1052
  13.1 0.0 copy-done.7
  13.1 3.8 %collective-permute-start.7 = (f32[19,32,128]{2,1,0:T(8,128)S(1)}, f32[19,32,128]{2,1,0:T(8,128)S(1)}, u32[]{:S(2)}, u32[]{:S(2)}) collective-permute-start(f32[19,32,128]{2,1,0:T(8,128)S(1)} %copy-done.7), channel_id=1, source_target_pairs={{0,8},{1,9},{2,10},{3,11},{4,12},{5,13},{6,14},{7,15},{8,0},{9,1},... | collective-permute-start | bytes 933896 | tf_op jit(solution)/shard_map/ppermute | solution.py:1045
  16.9 0.0 copy-done.6
  16.9 0.7 collective-permute-start.8
  17.6 0.0 copy-done.3
  17.6 1.8 %shard_map.79 = (f32[3,16,32,128]{3,2,1,0:T(8,128)S(1)}, f32[8,128]{1,0:T(8,128)S(1)}) custom-call(f32[3,16,32,128]{3,2,1,0:T(8,128)S(1)} %bitcast.16, f32[3,3,16,32,128]{4,3,2,1,0:T(8,128)S(1)} %bitcast.11, f32[16,32,128]{2,1,0:T(8,128)S(1)} %bitcast.21, f32[3,16,32,128]{3,2,1,0:T(8,128)S(1)} %bitcast.23, ...), custom_call_target="tpu_custom_call" | custom-call | flops 20000000 | bytes 20000000 | tf_op jit(solution)/shard_map/pallas_call | solution.py:1093
  19.3 0.0 collective-permute-done.4.strain.unit.unit_old
  19.3 0.1 shard_map.81
  19.4 6.9 %collective-permute-start.5 = (f32[9,32,128]{2,1,0:T(8,128)S(1)}, f32[9,32,128]{2,1,0:T(8,128)S(1)}, u32[]{:S(2)}, u32[]{:S(2)}) collective-permute-start(f32[9,32,128]{2,1,0:T(8,128)S(1)} %get-tuple-element.46), channel_id=1, source_target_pairs={{0,8},{1,9},{2,10},{3,11},{4,12},{5,13},{6,14},{7,15},{8,0},{9,1},... | collective-permute-start | bytes 442376 | tf_op jit(solution)/shard_map/ppermute | solution.py:1045
  26.4 0.7 collective-permute-start.6
  27.0 0.0 collective-permute-done.7.fa
  27.0 0.0 collective-permute-done.8.fb
  27.1 2.8 %collective-permute-done.5.xa.refs_0_ = f32[9,32,128]{2,1,0:T(8,128)S(1)} collective-permute-done((f32[9,32,128]{2,1,0:T(8,128)S(1)}, f32[9,32,128]{2,1,0:T(8,128)S(1)}, u32[]{:S(2)}, u32[]{:S(2)}) %collective-permute-start.5) | collective-permute-done | bytes 147488 | tf_op jit(solution)/shard_map/ppermute | solution.py:1045
  29.8 0.0 collective-permute-done.6.xb.refs_1_
  29.8 0.3 shard_map.82
  30.1 2.7 %collective-permute-start.9 = (f32[280,128]{1,0:T(8,128)S(1)}, f32[280,128]{1,0:T(8,128)S(1)}, u32[]{:S(2)}, u32[]{:S(2)}) collective-permute-start(f32[280,128]{1,0:T(8,128)S(1)} %get-tuple-element.50), channel_id=1, source_target_pairs={{0,1},{1,0},{2,3},{3,2},{4,5},{5,4},{6,7},{7,6},{8,9},{9,8},{10,11... | collective-permute-start | bytes 430088 | tf_op jit(solution)/shard_map/ppermute | solution.py:1045
  32.8 0.7 collective-permute-start.10
  33.4 1.2 %shard_map.83 = (f32[12,22,40,128]{3,2,1,0:T(8,128)S(1)}, f32[6,8,40,128]{3,2,1,0:T(8,128)S(1)}) custom-call(f32[3,3,16,32,128]{4,3,2,1,0:T(8,128)S(1)} %bitcast.12, f32[16,32,128]{2,1,0:T(8,128)S(1)} %bitcast.22, f32[3,16,32,128]{3,2,1,0:T(8,128)S(1)} %get-tuple-element.52.tz, s32[1,384]{1,0:T(1,128)S(1)} %reshape.9.layer_map, ...), custom_call_target="tpu_custom_call" | custom-call | flops 30000000 | bytes 30000000 | tf_op jit(solution)/shard_map/pallas_call | solution.py:1099
  34.6 0.7 collective-permute-done.9.refs_2_
  35.3 0.0 collective-permute-done.10.refs_3_
  35.3 2.4 %shard_map.84 = (f32[12,6,40,128]{3,2,1,0:T(8,128)S(1)}, f32[3,22,40,128]{3,2,1,0:T(8,128)S(1)}, f32[3,22,40,128]{3,2,1,0:T(8,128)S(1)}, f32[2,20,40,128]{3,2,1,0:T(8,128)S(1)}) custom-call(f32[3,16,32,128]{3,2,1,0:T(8,128)S(1)} %get-tuple-element.44.residual, f32[16,32,128]{2,1,0:T(8,128)S(1)} %collective-permute-done.4.strain.unit.unit_old, ...), custom_call_target="tpu_custom_call" | custom-call | tf_op jit(solution)/shard_map/pallas_call | solution.py:1110
  37.7 2.5 %collective-permute-start.11 = (f32[2,20,40,128]{3,2,1,0:T(8,128)S(1)}, f32[2,20,40,128]{3,2,1,0:T(8,128)S(1)}, u32[]{:S(2)}, u32[]{:S(2)}) collective-permute-start(f32[2,20,40,128]{3,2,1,0:T(8,128)S(1)} %get-tuple-element.58), channel_id=1, source_target_pairs={{0,64},{1,65},{2,66},{3,67},{4,68},{5,69},{6,70},{7,71},{8,72},{9,... | collective-permute-start | bytes 2457608 | tf_op jit(solution)/shard_map/ppermute | solution.py:1052
  40.2 1.1 %shard_map.85.sums_in = f32[8,128]{1,0:T(8,128)S(1)} custom-call(f32[3,22,40,128]{3,2,1,0:T(8,128)S(1)} %get-tuple-element.55.field.refs_2_, f32[3,22,40,128]{3,2,1,0:T(8,128)S(1)} %get-tuple-element.56.product.refs_3_, f32[12,22,40,128]{3,2,1,0:T(8,128)S(1)} %get-tuple-element.53.refs_4_.faces, f32[3,16,32,128]{3,2,1,0:T(8,128)S(1)} %bitcast.17), custom_call_target="tpu_custom_call" | custom-call | flops 20000000 | bytes 20000000 | tf_op jit(solution)/shard_map/pallas_call | solution.py:1116
  41.3 0.8 %collective-permute-done.11.unit = f32[2,20,40,128]{3,2,1,0:T(8,128)S(1)} collective-permute-done((f32[2,20,40,128]{3,2,1,0:T(8,128)S(1)}, f32[2,20,40,128]{3,2,1,0:T(8,128)S(1)}, u32[]{:S(2)}, u32[]{:S(2)}) %collective-permute-start.11) | collective-permute-done | bytes 819232 | tf_op jit(solution)/shard_map/ppermute | solution.py:1052
  42.2 7.2 %shard_map.86 = (f32[128,128]{1,0:T(8,128)S(1)}, f32[2,3,22,40,128]{4,3,2,1,0:T(8,128)S(1)}, f32[2,3,22,40,128]{4,3,2,1,0:T(8,128)S(1)}) custom-call(f32[3,22,40,128]{3,2,1,0:T(8,128)S(1)} %get-tuple-element.55.field.refs_2_, f32[3,22,40,128]{3,2,1,0:T(8,128)S(1)} %get-tuple-element.56.product.refs_3_, ...), custom_call_target="tpu_custom_call" | custom-call | tf_op jit(solution)/shard_map/pallas_call | solution.py:1119
  49.4 29.2 %all_to_all.11 = f32[128,1,128]{2,1,0:T(1,128)S(1)} all-to-all(f32[128,1,128]{2,1,0:T(1,128)S(1)} %bitcast.25), channel_id=1, replica_groups=mesh['group'=2,'gx'=8,'gy'=8] {'group','gx','gy'}, dimensions={0} | all-to-all | bytes 131072 | tf_op jit(solution)/shard_map/all_to_all | solution.py:1124
  78.6 1.9 %shard_map.87 = (f32[3,16,32,128]{3,2,1,0:T(8,128)}, f32[2]{0:T(128)}) custom-call(f32[128,128]{1,0:T(8,128)S(1)} %bitcast.24, f32[3,16,32,128]{3,2,1,0:T(8,128)S(1)} %bitcast.18, f32[3,22,40,128]{3,2,1,0:T(8,128)S(1)} %get-tuple-element.55.field.refs_2_, f32[3,22,40,128]{3,2,1,0:T(8,128)S(1)} %get-tuple-element.56.product.refs_3_, ...), custom_call_target="tpu_custom_call" | custom-call | tf_op jit(solution)/shard_map/pallas_call | solution.py:1129
  (1 shorter events, 0.0 us)
Async XLA Ops:
  0.6 8.3 %copy-start.4 = (s32[16,32]{1,0:T(8,128)S(1)}, s32[16,32]{1,0:T(8,128)}, u32[]{:S(2)}) copy-start(s32[16,32]{1,0:T(8,128)} %flags_in.1) | copy-start | bytes 6148
  0.6 8.3 %copy-start.2 = (f32[1,16,32,128]{3,2,1,0:T(8,128)S(1)}, f32[1,16,32,128]{3,2,1,0:T(8,128)}, u32[]{:S(2)}) copy-start(f32[1,16,32,128]{3,2,1,0:T(8,128)} %param.8) | copy-start | bytes 786436
  0.7 8.3 %copy-start = (f32[1,3,3,16,32,128]{5,4,3,2,1,0:T(8,128)S(1)}, f32[1,3,3,16,32,128]{5,4,3,2,1,0:T(8,128)}, u32[]{:S(2)}) copy-start(f32[1,3,3,16,32,128]{5,4,3,2,1,0:T(8,128)} %param.7) | copy-start | bytes 7077892
  0.7 8.3 %copy-start.1 = (f32[1,3,16,32,128]{4,3,2,1,0:T(8,128)S(1)}, f32[1,3,16,32,128]{4,3,2,1,0:T(8,128)}, u32[]{:S(2)}) copy-start(f32[1,3,16,32,128]{4,3,2,1,0:T(8,128)} %param.6) | copy-start | bytes 2359300
  0.7 8.2 %copy-start.5 = (s32[384]{0:T(512)S(1)}, s32[384]{0:T(512)}, u32[]{:S(2)}) copy-start(s32[384]{0:T(512)} %param.11) | copy-start | bytes 4612
  4.0 9.1 %copy-start.7 = (f32[19,32,128]{2,1,0:T(8,128)S(1)}, f32[19,32,128]{2,1,0:T(8,128)}, u32[]{:S(2)}) copy-start(f32[19,32,128]{2,1,0:T(8,128)} %get-tuple-element.48) | copy-start | bytes 933892
  4.0 12.8 %copy-start.6 = (f32[19,32,128]{2,1,0:T(8,128)S(1)}, f32[19,32,128]{2,1,0:T(8,128)}, u32[]{:S(2)}) copy-start(f32[19,32,128]{2,1,0:T(8,128)} %get-tuple-element.49) | copy-start | bytes 933892
  4.0 13.5 %copy-start.3 = (f32[1,3,16,32,128]{4,3,2,1,0:T(8,128)S(1)}, f32[1,3,16,32,128]{4,3,2,1,0:T(8,128)}, u32[]{:S(2)}) copy-start(f32[1,3,16,32,128]{4,3,2,1,0:T(8,128)} %param.9) | copy-start | bytes 2359300
  4.1 7.1 %collective-permute-start.2 = (f32[26,16,128]{2,1,0:T(8,128)}, f32[26,16,128]{2,1,0:T(8,128)S(1)}, u32[]{:S(2)}, u32[]{:S(2)}) collective-permute-start(f32[26,16,128]{2,1,0:T(8,128)} %get-tuple-element.36), channel_id=1, source_target_pairs={{0,1},{1,0},{2,3},{3,2},{4,5},{5,4},{6,7},{7,6},{8,9},{9,8},{10,11... | collective-permute-start | bytes 638984 | tf_op jit(solution)/shard_map/ppermute | solution.py:1045
  6.3 4.9 %collective-permute-start.3 = (f32[26,16,128]{2,1,0:T(8,128)}, f32[26,16,128]{2,1,0:T(8,128)S(1)}, u32[]{:S(2)}, u32[]{:S(2)}) collective-permute-start(f32[26,16,128]{2,1,0:T(8,128)} %get-tuple-element.37), channel_id=1, source_target_pairs={{1,2},{2,1},{3,4},{4,3},{5,6},{6,5},{9,10},{10,9},{11,12},{12,11},... | collective-permute-start | bytes 638984 | tf_op jit(solution)/shard_map/ppermute | solution.py:1045
  6.9 4.2 %collective-permute-start = (f32[7,32,128]{2,1,0:T(8,128)}, f32[7,32,128]{2,1,0:T(8,128)S(1)}, u32[]{:S(2)}, u32[]{:S(2)}) collective-permute-start(f32[7,32,128]{2,1,0:T(8,128)} %get-tuple-element.34), channel_id=1, source_target_pairs={{0,8},{1,9},{2,10},{3,11},{4,12},{5,13},{6,14},{7,15},{8,0},{9,1},... | collective-permute-start | bytes 344072 | tf_op jit(solution)/shard_map/ppermute | solution.py:1045
  8.2 2.9 %collective-permute-start.1 = (f32[7,32,128]{2,1,0:T(8,128)}, f32[7,32,128]{2,1,0:T(8,128)S(1)}, u32[]{:S(2)}, u32[]{:S(2)}) collective-permute-start(f32[7,32,128]{2,1,0:T(8,128)} %get-tuple-element.35), channel_id=1, source_target_pairs={{8,16},{9,17},{10,18},{11,19},{12,20},{13,21},{14,22},{15,23},{16,... | collective-permute-start | bytes 344072 | tf_op jit(solution)/shard_map/ppermute | solution.py:1045
  11.3 8.0 %collective-permute-start.4 = (f32[16,32,128]{2,1,0:T(8,128)S(1)}, f32[16,32,128]{2,1,0:T(8,128)S(1)}, u32[]{:S(2)}, u32[]{:S(2)}) collective-permute-start(f32[16,32,128]{2,1,0:T(8,128)S(1)} %shard_map.80), channel_id=1, source_target_pairs={{0,64},{1,65},{2,66},{3,67},{4,68},{5,69},{6,70},{7,71},{8,72},{9,... | collective-permute-start | bytes 786440 | tf_op jit(solution)/shard_map/ppermute | solution.py:1052
  13.1 13.9 %collective-permute-start.7 = (f32[19,32,128]{2,1,0:T(8,128)S(1)}, f32[19,32,128]{2,1,0:T(8,128)S(1)}, u32[]{:S(2)}, u32[]{:S(2)}) collective-permute-start(f32[19,32,128]{2,1,0:T(8,128)S(1)} %copy-done.7), channel_id=1, source_target_pairs={{0,8},{1,9},{2,10},{3,11},{4,12},{5,13},{6,14},{7,15},{8,0},{9,1},... | collective-permute-start | bytes 933896 | tf_op jit(solution)/shard_map/ppermute | solution.py:1045
  16.9 10.2 %collective-permute-start.8 = (f32[19,32,128]{2,1,0:T(8,128)S(1)}, f32[19,32,128]{2,1,0:T(8,128)S(1)}, u32[]{:S(2)}, u32[]{:S(2)}) collective-permute-start(f32[19,32,128]{2,1,0:T(8,128)S(1)} %copy-done.6), channel_id=1, source_target_pairs={{8,16},{9,17},{10,18},{11,19},{12,20},{13,21},{14,22},{15,23},{16,... | collective-permute-start | bytes 933896 | tf_op jit(solution)/shard_map/ppermute | solution.py:1045
  19.4 10.4 %collective-permute-start.5 = (f32[9,32,128]{2,1,0:T(8,128)S(1)}, f32[9,32,128]{2,1,0:T(8,128)S(1)}, u32[]{:S(2)}, u32[]{:S(2)}) collective-permute-start(f32[9,32,128]{2,1,0:T(8,128)S(1)} %get-tuple-element.46), channel_id=1, source_target_pairs={{0,8},{1,9},{2,10},{3,11},{4,12},{5,13},{6,14},{7,15},{8,0},{9,1},... | collective-permute-start | bytes 442376 | tf_op jit(solution)/shard_map/ppermute | solution.py:1045
  26.4 3.4 %collective-permute-start.6 = (f32[9,32,128]{2,1,0:T(8,128)S(1)}, f32[9,32,128]{2,1,0:T(8,128)S(1)}, u32[]{:S(2)}, u32[]{:S(2)}) collective-permute-start(f32[9,32,128]{2,1,0:T(8,128)S(1)} %get-tuple-element.47), channel_id=1, source_target_pairs={{8,16},{9,17},{10,18},{11,19},{12,20},{13,21},{14,22},{15,23},{16,... | collective-permute-start | bytes 442376 | tf_op jit(solution)/shard_map/ppermute | solution.py:1045
  30.1 5.2 %collective-permute-start.9 = (f32[280,128]{1,0:T(8,128)S(1)}, f32[280,128]{1,0:T(8,128)S(1)}, u32[]{:S(2)}, u32[]{:S(2)}) collective-permute-start(f32[280,128]{1,0:T(8,128)S(1)} %get-tuple-element.50), channel_id=1, source_target_pairs={{0,1},{1,0},{2,3},{3,2},{4,5},{5,4},{6,7},{7,6},{8,9},{9,8},{10,11... | collective-permute-start | bytes 430088 | tf_op jit(solution)/shard_map/ppermute | solution.py:1045
  32.8 2.5 %collective-permute-start.10 = (f32[280,128]{1,0:T(8,128)S(1)}, f32[280,128]{1,0:T(8,128)S(1)}, u32[]{:S(2)}, u32[]{:S(2)}) collective-permute-start(f32[280,128]{1,0:T(8,128)S(1)} %get-tuple-element.51), channel_id=1, source_target_pairs={{1,2},{2,1},{3,4},{4,3},{5,6},{6,5},{9,10},{10,9},{11,12},{12,11},... | collective-permute-start | bytes 430088 | tf_op jit(solution)/shard_map/ppermute | solution.py:1045
  37.7 4.5 %collective-permute-start.11 = (f32[2,20,40,128]{3,2,1,0:T(8,128)S(1)}, f32[2,20,40,128]{3,2,1,0:T(8,128)S(1)}, u32[]{:S(2)}, u32[]{:S(2)}) collective-permute-start(f32[2,20,40,128]{3,2,1,0:T(8,128)S(1)} %get-tuple-element.58), channel_id=1, source_target_pairs={{0,64},{1,65},{2,66},{3,67},{4,68},{5,69},{6,70},{7,71},{8,72},{9,... | collective-permute-start | bytes 2457608 | tf_op jit(solution)/shard_map/ppermute | solution.py:1052
